TPU v7x, 32 devices: a whole 2x2x4 slice. The times are simulated.
32 devices in a mesh: half: 2 (over x), dp: 16 (over z, y, core).
Axes of the slice: x: 2, y: 2, z: 4, core: 2. Of those that a mesh axis runs over, the one named last changes fastest.
Arguments:
- tokens: bfloat16 [2, 16, 1024, 512], P('half', 'dp'), may hold values from -6 to 6
- cotangent: float32 [2, 16, 1024, 512], P('half', 'dp'), may hold values from -6 to 6
- lengths: int32 [2, 16, 16], P(None, 'dp'), may hold values from 1 to 256, 1024 in all within a row
- halting: int32 [2, 16, 1024], P('half', 'dp'), may hold values 0 or 1
- attention_in: bfloat16 [2, 512, 1536], P('half'), may hold values from -0.25 to 0.25
- attention_out: bfloat16 [2, 512, 512], P('half'), may hold values from -1 to 1
- cross_first: bfloat16 [2, 512, 512], P('half'), may hold values from -0.25 to 0.25
- cross_second: bfloat16 [2, 512, 512], P('half'), may hold values from -0.5 to 0.5
- expand_weight: bfloat16 [2, 512, 2048], P('half'), may hold values from -0.25 to 0.25
- expand_bias: float32 [2, 2048], P('half'), may hold values from -3 to 3
- contract_weight: bfloat16 [2, 2048, 512], P('half'), may hold values from -0.125 to 0.125
- contract_bias: float32 [2, 512], P('half'), may hold values from -2 to 2
- norm_gain: float32 [2, 3, 512], P('half'), may hold values from 0.25 to 1.75
- norm_bias: float32 [2, 3, 512], P('half'), may hold values from -1.2 to 1.2
Outputs:
- outputs: float32 [2, 16, 1024, 512], P('half', 'dp')
- input_grad: float32 [2, 16, 1024, 512], P('half', 'dp')
- attention_in_grad: float32 [2, 512, 1536], P('half')
- attention_out_grad: float32 [2, 512, 512], P('half')
- cross_first_grad: float32 [2, 512, 512], P('half')
- cross_second_grad: float32 [2, 512, 512], P('half')
- expand_weight_grad: float32 [2, 512, 2048], P('half')
- expand_bias_grad: float32 [2, 2048], P('half')
- contract_weight_grad: float32 [2, 2048, 512], P('half')
- contract_bias_grad: float32 [2, 512], P('half')
- norm_gain_grad: float32 [2, 3, 512], P('half')
- norm_bias_grad: float32 [2, 3, 512], P('half')
All inputs are finite; a program needn't handle non-finite values. No bound on the sum of `halting` on one device may be relied on, other than what follows from the above.
Results may differ from a plain program's by a relative error of at most 0.024.
Values may be sent and summed in bfloat16 or wider, within the bound.
No kernel may reach another device: no remote copies, remote signals or barrier semaphores. Data moves between devices by JAX's collectives and lax.ppermute only.
A program may use at most 192 MiB of HBM per device.

v0:
```python
from functools import partial
import math

import jax
import jax.numpy as jnp
from jax import lax
from jax.sharding import PartitionSpec as P

HEADS = 8
STEP = 2


EPSILON = 1e-06


def from_behind(value, axis, by):
    count = lax.axis_size(axis)
    pairs = [(i, i + by) for i in range(count) if 0 <= i + by < count]
    return lax.ppermute(value, axis, pairs)


def layer_norm(summed, gain_row, shift_row):
    center = summed - jnp.mean(summed, axis=-1, keepdims=True)
    spread = jnp.mean(center * center, axis=-1, keepdims=True)
    return center * lax.rsqrt(spread + EPSILON) * gain_row + shift_row


def positions(lengths_row, length):
    endings = jnp.cumsum(lengths_row)
    places = jnp.arange(length, dtype=jnp.int32)
    passed = (places[:, None] >= endings[None, :]).astype(jnp.int32)
    segment = jnp.sum(passed, axis=1)
    begins = jnp.sum(passed * lengths_row[None, :], axis=1)
    return (segment, places - begins)


def timing(places, model_width):
    half_width = model_width // 2
    frequency = jnp.exp(
        jnp.arange(half_width, dtype=jnp.float32) * (-math.log(10000.0) / half_width)
    )
    angles = places[..., None] * frequency
    return jnp.concatenate([jnp.sin(angles), jnp.cos(angles)], axis=-1)


def smooth_gate(values_in):
    return jax.nn.gelu(values_in, approximate=True)


def masked_scores(
    query_block, key_heads, segment_block, key_segments, first_row, causal, score_scale
):
    scores = (
        jnp.einsum("bhd,khd->hbk", query_block, key_heads, preferred_element_type=jnp.float32)
        * score_scale
    )
    query_places = first_row + jnp.arange(query_block.shape[0], dtype=jnp.int32)
    key_places = jnp.arange(key_heads.shape[0], dtype=jnp.int32)
    allowed = (segment_block[:, None] == key_segments[None, :]) & (
        jnp.logical_not(causal) | (query_places[:, None] >= key_places[None, :])
    )
    return jnp.where(allowed[None], scores, -jnp.inf)


def attend_forward(queries, keys, values, query_segments, key_segments, causal, heads):
    length, model_width = queries.shape
    key_count = keys.shape[0]
    head_size = model_width // heads
    block_rows = min(512, length)
    block_count = length // block_rows
    score_scale = 1.0 / math.sqrt(head_size)
    key_heads = keys.reshape(key_count, heads, head_size)
    value_heads = values.reshape(key_count, heads, head_size)

    def one_block(packed):
        query_block, segment_block, first_row = packed
        scores = masked_scores(
            query_block, key_heads, segment_block, key_segments, first_row, causal, score_scale
        )
        row_max = jnp.max(scores, axis=-1, keepdims=True)
        exponent = jnp.exp(scores - row_max)
        row_total = jnp.sum(exponent, axis=-1, keepdims=True)
        attention_low = (exponent / row_total).astype(jnp.bfloat16)
        mixed_out = jnp.einsum(
            "hbk,khd->bhd", attention_low, value_heads, preferred_element_type=jnp.float32
        )
        return (mixed_out.reshape(block_rows, model_width), (row_max + jnp.log(row_total))[..., 0])

    starts = jnp.arange(block_count, dtype=jnp.int32) * block_rows
    mixed_out, log_totals = lax.map(
        one_block,
        (
            queries.reshape(block_count, block_rows, heads, head_size),
            query_segments.reshape(block_count, block_rows),
            starts,
        ),
    )
    return (mixed_out.reshape(length, model_width), log_totals)


def attend_backward(
    queries, keys, values, query_segments, key_segments, causal, heads, grad_mixed, log_totals
):
    length, model_width = queries.shape
    key_count = keys.shape[0]
    head_size = model_width // heads
    block_rows = min(512, length)
    block_count = length // block_rows
    score_scale = 1.0 / math.sqrt(head_size)
    key_heads = keys.reshape(key_count, heads, head_size)
    value_heads = values.reshape(key_count, heads, head_size)

    def one_block(carried, packed):
        key_total, value_total = carried
        query_block, segment_block, first_row, grad_block, log_block = packed
        scores = masked_scores(
            query_block, key_heads, segment_block, key_segments, first_row, causal, score_scale
        )
        attention_full = jnp.exp(scores - log_block[..., None])
        grad_attention = jnp.einsum(
            "bhd,khd->hbk", grad_block, value_heads, preferred_element_type=jnp.float32
        )
        row_inner = jnp.sum(attention_full * grad_attention, axis=-1, keepdims=True)
        grad_scores = (attention_full * (grad_attention - row_inner)).astype(jnp.bfloat16)
        grad_query = (
            jnp.einsum("hbk,khd->bhd", grad_scores, key_heads, preferred_element_type=jnp.float32)
            * score_scale
        )
        key_total = (
            key_total
            + jnp.einsum(
                "hbk,bhd->khd", grad_scores, query_block, preferred_element_type=jnp.float32
            )
            * score_scale
        )
        value_total = value_total + jnp.einsum(
            "hbk,bhd->khd",
            attention_full.astype(jnp.bfloat16),
            grad_block,
            preferred_element_type=jnp.float32,
        )
        return ((key_total, value_total), grad_query.reshape(block_rows, model_width))

    starts = jnp.arange(block_count, dtype=jnp.int32) * block_rows
    zero_heads = jnp.zeros((key_count, heads, head_size), jnp.float32)
    packed = (
        queries.reshape(block_count, block_rows, heads, head_size),
        query_segments.reshape(block_count, block_rows),
        starts,
        grad_mixed.reshape(block_count, block_rows, heads, head_size),
        log_totals,
    )
    (key_total, value_total), grad_query = lax.scan(one_block, (zero_heads, zero_heads), packed)
    return (
        grad_query.reshape(length, model_width),
        key_total.reshape(key_count, model_width),
        value_total.reshape(key_count, model_width),
    )


def ffn_pieces(inputs, weights):
    expand_w, expand_b, contract_w, contract_b = weights
    flat_rows = inputs.reshape(-1, inputs.shape[-1])
    low_in = flat_rows.astype(jnp.bfloat16)
    before = jnp.dot(low_in, expand_w, preferred_element_type=jnp.float32) + expand_b
    hidden = smooth_gate(before).astype(jnp.bfloat16)
    summed = (
        flat_rows + jnp.dot(hidden, contract_w, preferred_element_type=jnp.float32) + contract_b
    )
    return (low_in, before, hidden, summed)


def ffn_backward(pieces, norm_back, grad_next, weights):
    low_in, before, hidden, summed = pieces
    grad_summed, grad_gain, grad_shift = norm_back(grad_next.reshape(summed.shape))
    grad_branch = grad_summed.astype(jnp.bfloat16)
    grad_contract_b = jnp.sum(grad_branch, axis=0, dtype=jnp.float32)
    grad_contract_w = jnp.einsum(
        "nf,nd->fd", hidden, grad_branch, preferred_element_type=jnp.float32
    )
    grad_hidden = jnp.einsum(
        "nd,fd->nf", grad_branch, weights[2], preferred_element_type=jnp.float32
    )
    gate_value, gate_back = jax.vjp(smooth_gate, before)
    grad_before = gate_back(grad_hidden)[0].astype(jnp.bfloat16)
    grad_expand_b = jnp.sum(grad_before, axis=0, dtype=jnp.float32)
    grad_expand_w = jnp.einsum("nd,nf->df", low_in, grad_before, preferred_element_type=jnp.float32)
    grad_inputs = grad_summed + jnp.einsum(
        "nf,df->nd", grad_before, weights[0], preferred_element_type=jnp.float32
    )
    return (
        grad_inputs,
        (grad_expand_w, grad_expand_b, grad_contract_w, grad_contract_b, grad_gain, grad_shift),
    )


def body(
    tokens,
    cotangent,
    lengths,
    halting,
    attention_in,
    attention_out,
    cross_first,
    cross_second,
    expand_weight,
    expand_bias,
    contract_weight,
    contract_bias,
    norm_gain,
    norm_bias,
):
    section = lax.axis_index("half")
    encoding = section == 0
    causal = jnp.logical_not(encoding)
    rows_here, length, model_width = (tokens.shape[1], tokens.shape[2], tokens.shape[3])
    tokens_here = rows_here * length
    field_shape = (rows_here, length, model_width)
    own_lengths = lax.dynamic_index_in_dim(lengths, section, 0, keepdims=False)
    own_segments, own_places = jax.vmap(partial(positions, length=length))(own_lengths)
    source_segments, source_places = jax.vmap(partial(positions, length=length))(lengths[0])
    state = tokens[0].astype(jnp.float32)
    start = (
        state
        + timing(own_places.astype(jnp.float32), model_width)
        + timing(jnp.float32(STEP), model_width)
    )
    running = halting[0].astype(jnp.float32)[..., None]
    weight_in = attention_in[0]
    weight_mix = attention_out[0]
    weight_first = cross_first[0]
    weight_second = cross_second[0]
    ffn_weights = (expand_weight[0], expand_bias[0], contract_weight[0], contract_bias[0])
    gain_rows = norm_gain[0]
    shift_rows = norm_bias[0]
    start_low = start.astype(jnp.bfloat16).reshape(tokens_here, model_width)
    projected = (
        jnp.dot(start_low, weight_in, preferred_element_type=jnp.float32)
        .astype(jnp.bfloat16)
        .reshape(rows_here, length, 3 * model_width)
    )

    def self_forward(packed):
        row_projected, row_segments = packed
        return attend_forward(
            row_projected[:, :model_width],
            row_projected[:, model_width : 2 * model_width],
            row_projected[:, 2 * model_width :],
            row_segments,
            row_segments,
            causal,
            HEADS,
        )

    attended, self_logs = lax.map(self_forward, (projected, own_segments))
    attended_low = attended.astype(jnp.bfloat16).reshape(tokens_here, model_width)
    first_sum = start + jnp.dot(
        attended_low, weight_mix, preferred_element_type=jnp.float32
    ).reshape(field_shape)
    after_self, first_back = jax.vjp(layer_norm, first_sum, gain_rows[0], shift_rows[0])

    def encode_tail(normed_in):
        tail_out = layer_norm(
            ffn_pieces(normed_in, ffn_weights)[3], gain_rows[1], shift_rows[1]
        ).reshape(field_shape)
        stepped = state + running * (tail_out - state)
        memory = layer_norm(stepped, gain_rows[2], shift_rows[2])
        memory_low = memory.astype(jnp.bfloat16).reshape(tokens_here, model_width)
        key_values = jnp.concatenate(
            [
                jnp.dot(memory_low, weight_first, preferred_element_type=jnp.float32),
                jnp.dot(memory_low, weight_second, preferred_element_type=jnp.float32),
            ],
            axis=-1,
        )
        return (memory, key_values.astype(jnp.bfloat16).reshape(rows_here, length, 2 * model_width))

    def skip_encode(normed_in):
        return (
            jnp.zeros_like(normed_in),
            jnp.zeros((rows_here, length, 2 * model_width), jnp.bfloat16),
        )

    result, key_values = lax.cond(encoding, encode_tail, skip_encode, after_self)
    arrived = from_behind(key_values, "half", 1)

    def cross_forward(normed_in, pairs_in):
        normed_low = normed_in.astype(jnp.bfloat16).reshape(tokens_here, model_width)
        queries = (
            jnp.dot(normed_low, weight_first, preferred_element_type=jnp.float32)
            .astype(jnp.bfloat16)
            .reshape(field_shape)
        )

        def row_cross(packed):
            row_query, row_pairs, row_segments, row_sources = packed
            return attend_forward(
                row_query,
                row_pairs[:, :model_width],
                row_pairs[:, model_width:],
                row_segments,
                row_sources,
                False,
                HEADS,
            )

        crossed, cross_logs = lax.map(row_cross, (queries, pairs_in, own_segments, source_segments))
        crossed_low = crossed.astype(jnp.bfloat16).reshape(tokens_here, model_width)
        second_sum = normed_in + jnp.dot(
            crossed_low, weight_second, preferred_element_type=jnp.float32
        ).reshape(field_shape)
        return (normed_low, queries, cross_logs, crossed_low, second_sum)

    def decode_tail(operands):
        normed_in, pairs_in, earlier = operands
        second_sum = cross_forward(normed_in, pairs_in)[4]
        second = layer_norm(second_sum, gain_rows[2], shift_rows[2])
        tail_out = layer_norm(
            ffn_pieces(second, ffn_weights)[3], gain_rows[1], shift_rows[1]
        ).reshape(field_shape)
        return state + running * (tail_out - state)

    def keep_result(operands):
        return operands[2]

    result = lax.cond(encoding, keep_result, decode_tail, (after_self, arrived, result))
    grad_out = cotangent[0]
    zero_field = jnp.zeros(field_shape, jnp.float32)
    zero_grads = (
        jnp.zeros(weight_first.shape, jnp.float32),
        jnp.zeros(weight_second.shape, jnp.float32),
        jnp.zeros(expand_weight.shape[1:], jnp.float32),
        jnp.zeros(expand_bias.shape[1:], jnp.float32),
        jnp.zeros(contract_weight.shape[1:], jnp.float32),
        jnp.zeros(contract_bias.shape[1:], jnp.float32),
        jnp.zeros((model_width,), jnp.float32),
        jnp.zeros((model_width,), jnp.float32),
        jnp.zeros((model_width,), jnp.float32),
        jnp.zeros((model_width,), jnp.float32),
    )

    def decode_back(normed_in):
        normed_low, queries, cross_logs, crossed_low, second_sum = cross_forward(normed_in, arrived)
        second, second_back = jax.vjp(layer_norm, second_sum, gain_rows[2], shift_rows[2])
        pieces = ffn_pieces(second, ffn_weights)
        tail_out, norm_back = jax.vjp(layer_norm, pieces[3], gain_rows[1], shift_rows[1])
        grad_inputs, ffn_grads = ffn_backward(pieces, norm_back, running * grad_out, ffn_weights)
        grad_second, grad_gain_two, grad_shift_two = second_back(grad_inputs.reshape(field_shape))
        grad_cross = grad_second.astype(jnp.bfloat16).reshape(tokens_here, model_width)
        grad_second_w = jnp.einsum(
            "nd,ne->de", crossed_low, grad_cross, preferred_element_type=jnp.float32
        )
        grad_crossed = (
            jnp.einsum("ne,de->nd", grad_cross, weight_second, preferred_element_type=jnp.float32)
            .astype(jnp.bfloat16)
            .reshape(field_shape)
        )

        def row_back(packed):
            row_query, row_pairs, row_segments, row_sources, row_grad, row_logs = packed
            return attend_backward(
                row_query,
                row_pairs[:, :model_width],
                row_pairs[:, model_width:],
                row_segments,
                row_sources,
                False,
                HEADS,
                row_grad,
                row_logs,
            )

        grad_queries, grad_keys, grad_values = lax.map(
            row_back, (queries, arrived, own_segments, source_segments, grad_crossed, cross_logs)
        )
        grad_queries_low = grad_queries.astype(jnp.bfloat16).reshape(tokens_here, model_width)
        grad_first_w = jnp.einsum(
            "nd,ne->de", normed_low, grad_queries_low, preferred_element_type=jnp.float32
        )
        grad_normed = grad_second + jnp.einsum(
            "ne,de->nd", grad_queries_low, weight_first, preferred_element_type=jnp.float32
        ).reshape(field_shape)
        grad_pairs = jnp.concatenate([grad_keys, grad_values], axis=-1).astype(jnp.bfloat16)
        return (
            grad_normed,
            (1.0 - running) * grad_out,
            (grad_first_w, grad_second_w) + ffn_grads + (grad_gain_two, grad_shift_two),
            grad_pairs,
        )

    def skip_decode_back(normed_in):
        return (
            zero_field,
            zero_field,
            zero_grads,
            jnp.zeros((rows_here, length, 2 * model_width), jnp.bfloat16),
        )

    grad_after, grad_direct, tail_grads, grad_pairs = lax.cond(
        encoding, skip_decode_back, decode_back, after_self
    )
    grad_arrived = from_behind(grad_pairs, "half", -1)

    def encode_back(operands):
        normed_in, pairs_grad, earlier = operands
        pieces = ffn_pieces(normed_in, ffn_weights)
        tail_out, norm_back = jax.vjp(layer_norm, pieces[3], gain_rows[1], shift_rows[1])
        stepped = state + running * (tail_out.reshape(field_shape) - state)
        memory, memory_back = jax.vjp(layer_norm, stepped, gain_rows[2], shift_rows[2])
        memory_low = memory.astype(jnp.bfloat16).reshape(tokens_here, model_width)
        grad_keys = pairs_grad[..., :model_width].reshape(tokens_here, model_width)
        grad_values = pairs_grad[..., model_width:].reshape(tokens_here, model_width)
        cross_part = jnp.einsum(
            "ne,de->nd", grad_keys, weight_first, preferred_element_type=jnp.float32
        ) + jnp.einsum("ne,de->nd", grad_values, weight_second, preferred_element_type=jnp.float32)
        grad_memory = grad_out + cross_part.reshape(field_shape)
        grad_first_w = jnp.einsum(
            "nd,ne->de", memory_low, grad_keys, preferred_element_type=jnp.float32
        )
        grad_second_w = jnp.einsum(
            "nd,ne->de", memory_low, grad_values, preferred_element_type=jnp.float32
        )
        grad_stepped, grad_gain_two, grad_shift_two = memory_back(grad_memory)
        grad_inputs, ffn_grads = ffn_backward(
            pieces, norm_back, running * grad_stepped, ffn_weights
        )
        return (
            grad_inputs.reshape(field_shape),
            (1.0 - running) * grad_stepped,
            (grad_first_w, grad_second_w) + ffn_grads + (grad_gain_two, grad_shift_two),
        )

    def keep_decoded(operands):
        return operands[2]

    grad_after, grad_direct, tail_grads = lax.cond(
        encoding,
        encode_back,
        keep_decoded,
        (after_self, grad_arrived, (grad_after, grad_direct, tail_grads)),
    )
    (
        tail_first_w,
        tail_second_w,
        tail_expand_w,
        tail_expand_b,
        tail_contract_w,
        tail_contract_b,
        tail_gain_one,
        tail_shift_one,
        tail_gain_two,
        tail_shift_two,
    ) = tail_grads
    grad_first, grad_gain_zero, grad_shift_zero = first_back(grad_after)
    grad_mix_low = grad_first.astype(jnp.bfloat16).reshape(tokens_here, model_width)
    grad_weight_mix = jnp.einsum(
        "nd,ne->de", attended_low, grad_mix_low, preferred_element_type=jnp.float32
    )
    grad_attended = (
        jnp.einsum("ne,de->nd", grad_mix_low, weight_mix, preferred_element_type=jnp.float32)
        .astype(jnp.bfloat16)
        .reshape(field_shape)
    )

    def self_back(packed):
        row_projected, row_segments, row_grad, row_logs = packed
        return attend_backward(
            row_projected[:, :model_width],
            row_projected[:, model_width : 2 * model_width],
            row_projected[:, 2 * model_width :],
            row_segments,
            row_segments,
            causal,
            HEADS,
            row_grad,
            row_logs,
        )

    grad_queries, grad_keys, grad_values = lax.map(
        self_back, (projected, own_segments, grad_attended, self_logs)
    )
    grad_projected = (
        jnp.concatenate([grad_queries, grad_keys, grad_values], axis=-1)
        .astype(jnp.bfloat16)
        .reshape(tokens_here, 3 * model_width)
    )
    grad_weight_in = jnp.einsum(
        "nd,ne->de", start_low, grad_projected, preferred_element_type=jnp.float32
    )
    grad_start = grad_first + jnp.einsum(
        "ne,de->nd", grad_projected, weight_in, preferred_element_type=jnp.float32
    ).reshape(field_shape)
    input_grad = grad_start + grad_direct
    (
        grad_weight_in,
        grad_weight_mix,
        grad_gain_zero,
        grad_shift_zero,
        tail_first_w,
        tail_second_w,
        tail_expand_w,
        tail_expand_b,
        tail_contract_w,
        tail_contract_b,
        tail_gain_one,
        tail_shift_one,
        tail_gain_two,
        tail_shift_two,
    ) = lax.psum(
        (
            grad_weight_in,
            grad_weight_mix,
            grad_gain_zero,
            grad_shift_zero,
            tail_first_w,
            tail_second_w,
            tail_expand_w,
            tail_expand_b,
            tail_contract_w,
            tail_contract_b,
            tail_gain_one,
            tail_shift_one,
            tail_gain_two,
            tail_shift_two,
        ),
        "dp",
    )
    gain_grads = jnp.stack([grad_gain_zero, tail_gain_one, tail_gain_two])
    shift_grads = jnp.stack([grad_shift_zero, tail_shift_one, tail_shift_two])
    return (
        result[None],
        input_grad[None],
        grad_weight_in[None],
        grad_weight_mix[None],
        tail_first_w[None],
        tail_second_w[None],
        tail_expand_w[None],
        tail_expand_b[None],
        tail_contract_w[None],
        tail_contract_b[None],
        gain_grads[None],
        shift_grads[None],
    )


def solution(mesh):
    placed = (
        P("half", "dp", None, None),
        P("half", "dp", None, None),
        P(None, "dp", None),
        P("half", "dp", None),
        P("half", None, None),
        P("half", None, None),
        P("half", None, None),
        P("half", None, None),
        P("half", None, None),
        P("half", None),
        P("half", None, None),
        P("half", None),
        P("half", None, None),
        P("half", None, None),
    )
    return jax.shard_map(
        body,
        mesh=mesh,
        in_specs=placed,
        out_specs=(
            P("half", "dp", None, None),
            P("half", "dp", None, None),
            P("half", None, None),
            P("half", None, None),
            P("half", None, None),
            P("half", None, None),
            P("half", None, None),
            P("half", None),
            P("half", None, None),
            P("half", None),
            P("half", None, None),
            P("half", None, None),
        ),
        check_vma=False,
    )
```

profile of v0, /device:TPU:0, one launch (start us, length us, event | category | flops | bytes accessed | tf_op | source)
XLA Modules:
  0.0 962.4 jit_solution(15994414802509195669)
XLA Ops:
  11.6 4.8 multiply_sine_fusion
  16.4 4.8 multiply_sine_fusion.1
  41.7 36.1 %while.118 = (s32[]{:T(128)}, bf16[2,512,512]{2,1,0:T(8,128)(2,1)}, f32[2,8,512]{2,1,0:T(8,128)S(1)}, s32[2,512]{1,0:T(2,128)S(1)}, s32[1024]{0:T(1024)S(1)}, /*...) while((s32[]{:T(128)}, bf16[2,512,512]{2,1,0:T(8,128)(2,1)}, ...), condition=%wide.region_6.7_spmd, body=%wide.region_3.6_spmd.sunk | while | flops 1126167040 | bytes 62011568 | solution.py:90
  47.8 4.2 fusion.349
  52.0 5.8 fusion.350
  65.8 4.2 fusion.349
  70.0 5.8 fusion.350
  84.2 23.6 %conditional.4 = (bf16[1,1024,1024]{1,2,0:T(8,128)(2,1)}, f32[1,1024,512]{1,2,0:T(8,128)}) conditional(s32[]{:T(128)} %convert_element_type.261, () %tuple.103, (f32[1,1024,1]{1,2,0:T(1,128)S(1)}, f32[1,1024,512]{1,2,0:T(8,128)}, bf16[512,2048]{1,0:T(8,128)(2,1)}, f32[1,2048]{1,0:T(1,128)S(1)}, bf16[2048,512]{1,0:T(8,128)(2,1)}, ...), branch_computations={%region_9.10_spmd, %region_10.15_spmd} | conditional | flops 5406984192 | bytes 43104300 | solution.py:284
  84.3 10.5 %fusion.227 = (f32[1024]{0:T(1024)S(1)}, f32[1024,512]{0,1:T(8,128)}) fusion(f32[512]{0:T(512)S(1)} %bitcast.656, bf16[2048,512]{1,0:T(8,128)(2,1)} %get-tuple-element.703, f32[2048]{0:T(1024)S(1)} %bitcast.650, bf16[512,2048]{1,0:T(8,128)(2,1)} %get-tuple-element.701, f32[1,1024,512]{1,2,0:T(8,128)} %get-tuple-element.700), kind=kOutput, calls=%fused_computation.379 | convolution fusion | flops 4317510656 | bytes 8402944 | tf_op jit(solution)/shard_map/cond/branch_1_fun/dot_general | solution.py:168
  111.3 43.9 %collective-permute-done = bf16[1,1024,1024]{1,2,0:T(8,128)(2,1)} collective-permute-done((bf16[1,1024,1024]{1,2,0:T(8,128)(2,1)}, bf16[1,1024,1024]{1,2,0:T(8,128)(2,1)}, u32[]{:S(2)}, u32[]{:S(2)}) %collective-permute-start) | collective-permute-done | bytes 2097184 | tf_op jit(solution)/shard_map/ppermute | solution.py:19
  155.2 22.9 %conditional.6 = (f32[1,1024,512]{1,2,0:T(8,128)}, f32[1,1024,512]{1,2,0:T(8,128)}, f32[512,512]{0,1:T(8,128)S(1)}, f32[512,512]{1,0:T(8,128)}, f32[512,2048]{1,...) conditional(s32[]{:T(128)} %convert_element_type.261, ...), branch_computations={%region_27.49_spmd, %region_49.50_spmd} | conditional | flops 20070273024 | bytes 584193344 | solution.py:399
  180.4 4.1 copy.164
  185.8 257.5 %collective-permute-done.1 = bf16[1,1024,1024]{2,1,0:T(8,128)(2,1)} collective-permute-done((bf16[1,1024,1024]{2,1,0:T(8,128)(2,1)}, bf16[1,1024,1024]{2,1,0:T(8,128)(2,1)}, u32[]{:S(2)}, u32[]{:S(2)}) %collective-permute-start.1) | collective-permute-done | bytes 2097184 | tf_op jit(solution)/shard_map/ppermute | solution.py:19
  443.4 80.5 %conditional.7 = (f32[512,512]{1,0:T(8,128)S(1)}, f32[512,512]{1,0:T(8,128)}, f32[2048]{0:T(1024)}, f32[2048,512]{1,0:T(8,128)}, f32[512]{0:T(512)}, /*index=5*/...) conditional(s32[]{:T(128)} %convert_element_type.261, ...), branch_computations={%region_50.51_spmd.clone, %region_51.0_spmd.clone} | conditional | flops 15139874816 | bytes 281323968 | solution.py:436
  451.4 8.0 multiply_convert_fusion.2
  480.7 4.1 fusion.108
  488.9 10.5 %convert_reduce_fusion = (f32[2048]{0:T(1024)}, bf16[1024,2048]{1,0:T(8,128)(2,1)S(1)}) fusion(f32[1024,2048]{1,0:T(8,128)} %get-tuple-element.1641, f32[2048]{0:T(1024)S(1)} %bitcast.654, bf16[1024,512]{1,0:T(8,128)(2,1)S(1)} %get-tuple-element.1589, bf16[2048,512]{1,0:T(8,128)(2,1)S(1)} %copy-done.115), kind=kOutput, calls=%fused_computation.152 | convolution fusion | flops 2195716096 | bytes 15745024 | tf_op jit(solution)/shard_map/cond/branch_1_fun/nd,fd->nf/dot_general | solution.py:181
  503.9 4.4 fusion.245
  511.2 7.2 convolution_bitcast_fusion
  518.4 5.3 copy.212
  539.3 118.3 %while.119 = (s32[]{:T(128)}, f32[1024,8,64]{0,2,1:T(8,128)}, f32[1024,8,64]{0,2,1:T(8,128)}, bf16[2,512,512]{2,1,0:T(8,128)(2,1)}, bf16[2,512,8,64]{1,3,2,0:T(8...) while((s32[]{:T(128)}, f32[1024,8,64]{0,2,1:T(8,128)}, ...), condition=%wide.region_70.71_spmd.clone, body=%wide.region_68.70_spmd.clone.sunk | while | flops 2727342592 | bytes 281639296 | solution.py:153
  541.7 9.6 fusion.360
  551.3 12.4 %multiply_reduce_fusion.18 = (f32[8,512]{1,0:T(8,128)S(1)}, f32[8,512,1024]{2,1,0:T(8,128)}) fusion(f32[8,512,1024]{2,1,0:T(8,128)} %fusion.360, f32[8,512]{1,0:T(8,128)S(1)} %dynamic-slice_bitcast_fusion.4, bf16[1024,8,64]{0,2,1:T(8,128)(2,1)S(1)} %get-tuple-element.2221, bf16[2,512,8,64]{1,3,2,0:T(8,128)(2,1)S(1)} %copy-done.14, s32[]{:T(128)S(6)} %copy.366, ...), kind=kOutput, calls=%fused_computation.116.clone.1 | convolution fusion | flops 557838336 | bytes 35684356 | tf_op jit(solution)/shard_map/while/body/eval_jaxpr/while/body/eval_jaxpr/bhd,khd->hbk/dot_general | solution.py:54
  563.7 15.0 %multiply_convert_fusion.6 = bf16[8,512,1024]{2,1,0:T(8,128)(2,1)} fusion(f32[8,512,1024]{2,1,0:T(8,128)} %get-tuple-element.1967, f32[8,512,1024]{2,1,0:T(8,128)} %fusion.360, f32[8,512]{1,0:T(8,128)S(1)} %get-tuple-element.1968), kind=kLoop, calls=%fused_computation.115.clone.1 | loop fusion | flops 12582912 | bytes 41959424 | tf_op jit(solution)/shard_map/while/body/eval_jaxpr/while/body/eval_jaxpr/convert_element_type | solution.py:124
  585.8 7.6 convolution_multiply_fusion.4
  600.6 9.6 fusion.360
  610.2 12.4 %multiply_reduce_fusion.18 = (f32[8,512]{1,0:T(8,128)S(1)}, f32[8,512,1024]{2,1,0:T(8,128)}) fusion(f32[8,512,1024]{2,1,0:T(8,128)} %fusion.360, f32[8,512]{1,0:T(8,128)S(1)} %dynamic-slice_bitcast_fusion.4, bf16[1024,8,64]{0,2,1:T(8,128)(2,1)S(1)} %get-tuple-element.2221, bf16[2,512,8,64]{1,3,2,0:T(8,128)(2,1)S(1)} %copy-done.14, s32[]{:T(128)S(6)} %copy.366, ...), kind=kOutput, calls=%fused_computation.116.clone.1 | convolution fusion | flops 557838336 | bytes 35684356 | tf_op jit(solution)/shard_map/while/body/eval_jaxpr/while/body/eval_jaxpr/bhd,khd->hbk/dot_general | solution.py:54
  622.6 15.0 %multiply_convert_fusion.6 = bf16[8,512,1024]{2,1,0:T(8,128)(2,1)} fusion(f32[8,512,1024]{2,1,0:T(8,128)} %get-tuple-element.1967, f32[8,512,1024]{2,1,0:T(8,128)} %fusion.360, f32[8,512]{1,0:T(8,128)S(1)} %get-tuple-element.1968), kind=kLoop, calls=%fused_computation.115.clone.1 | loop fusion | flops 12582912 | bytes 41959424 | tf_op jit(solution)/shard_map/while/body/eval_jaxpr/while/body/eval_jaxpr/convert_element_type | solution.py:124
  644.7 7.6 convolution_multiply_fusion.4
  665.9 6.0 convolution_bitcast_fusion.2
  676.2 64.0 %all-reduce = (f32[1,2048]{1,0:T(1,128)}, f32[1,512]{1,0:T(1,128)}, f32[1,512]{1,0:T(1,128)S(1)}, f32[1,512]{1,0:T(1,128)S(1)}, f32[1,512]{1,0:T(1,128)S(1)}, /*...) all-reduce(f32[1,2048]{1,0:T(1,128)S(1)} %bitcast.629, ...), channel_id=1, replica_groups=mesh['half'=2,'dp'=16] {'dp'}, use_global_device_ids=true, to_apply=%region_76.77 | all-reduce | flops 5632 | bytes 45056 | tf_op jit(solution)/shard_map/psum | solution.py:509
  750.3 192.3 %all-reduce.4.cloned.1.call-done = (f32[1,512,1536]{2,1,0:T(8,128)}, f32[1,512,512]{2,1,0:T(8,128)}, f32[1,512,512]{2,1,0:T(8,128)}, f32[1,512,512]{2,1,0:T(8,12...) async-done(((f32[1,512,1536]{2,1,0:T(8,128)}, f32[1,512,512]{2,1,0:T(8,128)}, f32[1,512,512]{2,1,0:T(8,128)}, f32[1,512,512]{2,1,0:T(8,128)}, ...) | async-done | bytes 14680080 | tf_op jit(solution)/shard_map/psum | solution.py:509
  (351 shorter events, 202.0 us)
Async XLA Ops:
  7.2 17.8 %copy-start = (bf16[1,512,1536]{2,1,0:T(8,128)(2,1)S(1)}, bf16[1,512,1536]{2,1,0:T(8,128)(2,1)}, u32[]{:S(2)}) copy-start(bf16[1,512,1536]{2,1,0:T(8,128)(2,1)} %param.36) | copy-start | bytes 4718596
  7.2 935.4 %all-reduce.4.cloned.1.call-start = ((), (), s32[]{:S(2)}) async-start(), calls=%async_computation | async-start | bytes 29360128 | tf_op jit(solution)/shard_map/psum | solution.py:509
  11.6 9.6 copy-start.105
  41.7 36.2 %copy-start.93 = (f32[512]{0:T(512)S(1)}, f32[512]{0:T(512)}, u32[]{:S(2)}) copy-start(f32[512]{0:T(512)} %copy-done.92) | copy-start | bytes 6148
  77.9 77.3 %copy-start.63 = (s32[1024]{0:T(1024)}, s32[1024]{0:T(1024)S(1)}, u32[]{:S(2)}) copy-start(s32[1024]{0:T(1024)S(1)} %get-tuple-element.2273) | copy-start | bytes 12292
  84.2 26.2 %copy-start.110 = (s32[1,16]{1,0:T(1,128)S(1)}, s32[1,16]{1,0:T(1,128)}, u32[]{:S(2)}) copy-start(s32[1,16]{1,0:T(1,128)} %get-tuple-element.1673) | copy-start | bytes 196
  107.9 47.4 %collective-permute-start = (bf16[1,1024,1024]{1,2,0:T(8,128)(2,1)}, bf16[1,1024,1024]{1,2,0:T(8,128)(2,1)}, u32[]{:S(2)}, u32[]{:S(2)}) collective-permute-start(bf16[1,1024,1024]{1,2,0:T(8,128)(2,1)} %get-tuple-element.844), channel_id=1, source_target_pairs={{0,16},{1,17},{2,18},{3,19},{4,20},{5,21},{6,22},{7,23},{8,24},{9,... | collective-permute-start | bytes 6291464 | tf_op jit(solution)/shard_map/ppermute | solution.py:19
  180.4 262.9 %copy-start.29 = (bf16[1,512,512]{2,1,0:T(8,128)(2,1)S(1)}, bf16[1,512,512]{2,1,0:T(8,128)(2,1)}, u32[]{:S(2)}) copy-start(bf16[1,512,512]{2,1,0:T(8,128)(2,1)} %param.38) | copy-start | bytes 1572868
  180.4 262.9 %copy-start.37 = (bf16[1,512,512]{2,1,0:T(8,128)(2,1)S(1)}, bf16[1,512,512]{2,1,0:T(8,128)(2,1)}, u32[]{:S(2)}) copy-start(bf16[1,512,512]{2,1,0:T(8,128)(2,1)} %param.39) | copy-start | bytes 1572868
  180.4 262.9 %copy-start.75 = (f32[3,512]{1,0:T(4,128)S(1)}, f32[3,512]{1,0:T(4,128)}, u32[]{:S(2)}) copy-start(f32[3,512]{1,0:T(4,128)} %get-tuple-element.1681) | copy-start | bytes 18436
  180.4 262.9 %copy-start.80 = (f32[3,512]{1,0:T(4,128)S(1)}, f32[3,512]{1,0:T(4,128)}, u32[]{:S(2)}) copy-start(f32[3,512]{1,0:T(4,128)} %get-tuple-element.1680) | copy-start | bytes 18436
  180.4 262.9 %copy-start.117 = (f32[1,2048]{1,0:T(1,128)S(1)}, f32[1,2048]{1,0:T(1,128)}, u32[]{:S(2)}) copy-start(f32[1,2048]{1,0:T(1,128)} %param.41) | copy-start | bytes 24580
  180.4 262.9 %copy-start.121 = (f32[1,512]{1,0:T(1,128)S(1)}, f32[1,512]{1,0:T(1,128)}, u32[]{:S(2)}) copy-start(f32[1,512]{1,0:T(1,128)} %param.43) | copy-start | bytes 6148
  184.5 258.8 %collective-permute-start.1 = (bf16[1,1024,1024]{2,1,0:T(8,128)(2,1)}, bf16[1,1024,1024]{2,1,0:T(8,128)(2,1)}, u32[]{:S(2)}, u32[]{:S(2)}) collective-permute-start(bf16[1,1024,1024]{2,1,0:T(8,128)(2,1)} %copy.164), channel_id=1, source_target_pairs={{16,0},{17,1},{18,2},{19,3},{20,4},{21,5},{22,6},{23,7},{24,8},{25... | collective-permute-start | bytes 6291464 | tf_op jit(solution)/shard_map/ppermute | solution.py:19
  443.4 80.6 %copy-start.73 = (f32[1024]{0:T(1024)S(1)}, f32[1024]{0:T(1024)}, u32[]{:S(2)}) copy-start(f32[1024]{0:T(1024)} %copy-done.72) | copy-start | bytes 12292
  443.4 80.6 %copy-start.78 = (f32[1024]{0:T(1024)S(1)}, f32[1024]{0:T(1024)}, u32[]{:S(2)}) copy-start(f32[1024]{0:T(1024)} %copy-done.77) | copy-start | bytes 12292
  443.4 80.6 %copy-start.85 = (f32[1,1,512]{2,0,1:T(1,128)S(1)}, f32[1,1,512]{2,0,1:T(1,128)}, u32[]{:S(2)}) copy-start(f32[1,1,512]{2,0,1:T(1,128)} %slice.103) | copy-start | bytes 6148
  451.4 8.0 copy-start.114
  464.7 6.0 copy-start.26
  488.9 10.5 %copy-start.112 = (bf16[512,2048]{1,0:T(8,128)(2,1)S(1)}, bf16[512,2048]{1,0:T(8,128)(2,1)}, u32[]{:S(2)}) copy-start(bf16[512,2048]{1,0:T(8,128)(2,1)} %get-tuple-element.1442) | copy-start | bytes 6291460 | tf_op jit(solution)/shard_map/cond
  541.7 9.6 copy-start.14
  563.7 18.4 %copy-start.2 = (f32[8,512,1024]{2,1,0:T(8,128)S(1)}, f32[8,512,1024]{2,1,0:T(8,128)}, u32[]{:S(2)}) copy-start(f32[8,512,1024]{2,1,0:T(8,128)} %get-tuple-element.1967) | copy-start | bytes 50331652 | tf_op jit(solution)/shard_map/while/body/eval_jaxpr/while
  563.7 19.0 %copy-start.16 = (f32[1024,8,64]{0,2,1:T(8,128)S(1)}, f32[1024,8,64]{0,2,1:T(8,128)}, u32[]{:S(2)}) copy-start(f32[1024,8,64]{0,2,1:T(8,128)} %get-tuple-element.2199) | copy-start | bytes 6291460 | tf_op jit(solution)/shard_map/while/body/eval_jaxpr/while
  582.7 10.7 %copy-start.5 = (f32[1024,8,64]{0,2,1:T(8,128)S(1)}, f32[1024,8,64]{0,2,1:T(8,128)}, u32[]{:S(2)}) copy-start(f32[1024,8,64]{0,2,1:T(8,128)} %get-tuple-element.2198) | copy-start | bytes 6291460 | tf_op jit(solution)/shard_map/while/body/eval_jaxpr/while
  585.7 7.7 copy-start.17
  585.8 7.6 copy-start.4
  600.6 9.6 copy-start.14
  622.6 18.4 %copy-start.2 = (f32[8,512,1024]{2,1,0:T(8,128)S(1)}, f32[8,512,1024]{2,1,0:T(8,128)}, u32[]{:S(2)}) copy-start(f32[8,512,1024]{2,1,0:T(8,128)} %get-tuple-element.1967) | copy-start | bytes 50331652 | tf_op jit(solution)/shard_map/while/body/eval_jaxpr/while
  622.6 19.0 %copy-start.16 = (f32[1024,8,64]{0,2,1:T(8,128)S(1)}, f32[1024,8,64]{0,2,1:T(8,128)}, u32[]{:S(2)}) copy-start(f32[1024,8,64]{0,2,1:T(8,128)} %get-tuple-element.2199) | copy-start | bytes 6291460 | tf_op jit(solution)/shard_map/while/body/eval_jaxpr/while
  641.6 10.7 %copy-start.5 = (f32[1024,8,64]{0,2,1:T(8,128)S(1)}, f32[1024,8,64]{0,2,1:T(8,128)}, u32[]{:S(2)}) copy-start(f32[1024,8,64]{0,2,1:T(8,128)} %get-tuple-element.2198) | copy-start | bytes 6291460 | tf_op jit(solution)/shard_map/while/body/eval_jaxpr/while
  644.7 7.7 copy-start.17
  644.7 7.6 copy-start.4
  (71 other events, 207.2 us)
Sparse Core Ops, SparseCore 0:
  672.1 270.4 all-reduce.3
where the time goes:
time: 970 us; the launch traced here: 962 us
  waiting for transfers between devices  494 us (51%)
  matrix products  170 us (18%)
  local copies, waits for them, and re-layouts  115 us (12%)
  other arithmetic  89.2 us (9%)
  blocking collectives  64 us (7%)
  between operations  15.1 us (2%)
  loops' own time  11.6 us (1%)
    ppermute x2, waiting for transfers between devices, from_behind(): return lax.ppermute(value, axis, pairs)  301 us
    psum x1, waiting for transfers between devices, body(): lax.psum((grad_weight_in, grad_weight_mix, grad_gain_zero, grad_shift_zer...  192 us
    psum x1, blocking collectives, body(): lax.psum((grad_weight_in, grad_weight_mix, grad_gain_zero, grad_shift_zer...  64 us
    dot_general x4, matrix products, masked_scores(): jnp.einsum('bhd,khd->hbk', query_block, key_heads, preferred_element_type...  32.8 us
    convert_element_type x2, other arithmetic, one_block(): (attention_full * (grad_attention - row_inner)).astype(jnp.bfloat16)  30.1 us
    unnamed x150, local copies, waits for them, and re-layouts  27 us
  transfers between devices with their start and end apart: 3, of which 3 were waited for; matrix products, arithmetic and copies ran while one was open for 1% of the time, Pallas kernels for 0%

commit v1 on v0

v1 whole, which is shorter than its diff:
```python
from functools import partial
import math

import jax
import jax.numpy as jnp
from jax import lax
from jax.experimental import pallas as pl
from jax.experimental.pallas import tpu as pltpu
from jax.sharding import PartitionSpec as P

HEADS = 8
STEP = 2
EPSILON = 1e-06
LONGEST = 256
ROWS = 256
KEYS = 128
PIECE = 512
MASKED = -1e30
VMEM_BYTES = 60 * 1024 * 1024
F32 = jnp.float32
BF16 = jnp.bfloat16


def mul(left, right):
    return jnp.dot(left, right, preferred_element_type=F32)


def mul_nt(left, right):
    return lax.dot_general(left, right, (((1,), (1,)), ((), ())), preferred_element_type=F32)


def iota(shape, axis):
    return lax.broadcasted_iota(jnp.int32, shape, axis)


def norm_parts(summed):
    center = summed - jnp.mean(summed, axis=-1, keepdims=True)
    rate = lax.rsqrt(jnp.mean(center * center, axis=-1, keepdims=True) + EPSILON)
    return center * rate, rate


def norm_back(grad, unit, rate, gain):
    scaled = grad * gain
    return rate * (
        scaled
        - jnp.mean(scaled, axis=-1, keepdims=True)
        - unit * jnp.mean(scaled * unit, axis=-1, keepdims=True)
    )


def gate(before):
    inner = math.sqrt(2.0 / math.pi) * (before + 0.044715 * before * before * before)
    half_one = 0.5 * (1.0 + jnp.tanh(inner))
    return before * half_one


def gate_and_slope(before):
    scale = math.sqrt(2.0 / math.pi)
    square = before * before
    bent = jnp.tanh(scale * before * (1.0 + 0.044715 * square))
    half_one = 0.5 + 0.5 * bent
    slope = half_one + 0.5 * before * (1.0 - bent * bent) * (
        scale * (1.0 + 3 * 0.044715 * square)
    )
    return before * half_one, slope


def bounds(lengths, side, key_side, block, causal):
    first_row = block * ROWS
    last_row = first_row + ROWS - 1
    place = first_row + iota((1, ROWS), 1)
    low = jnp.zeros((1, ROWS), jnp.int32)
    high = jnp.zeros((1, ROWS), jnp.int32)
    least = jnp.int32(0)
    most = jnp.int32(0)
    at = jnp.int32(0)
    key_at = jnp.int32(0)
    for k in range(lengths.shape[1]):
        end = at + lengths[side, k]
        key_end = key_at + lengths[key_side, k]
        inside = (place >= at) & (place < end)
        low = jnp.where(inside, key_at, low)
        high = jnp.where(inside, key_end, high)
        least = jnp.where((first_row >= at) & (first_row < end), key_at, least)
        most = jnp.where((last_row >= at) & (last_row < end), key_end, most)
        at, key_at = end, key_end
    if causal is not None:
        high = jnp.where(causal, jnp.minimum(high, place + 1), high)
        most = jnp.where(causal, jnp.minimum(most, last_row + 1), most)
    return low, high, least // KEYS, (most + KEYS - 1) // KEYS


def keep_pair(block, axis):
    place = iota(block.shape, axis)
    half = block.shape[axis] // 2
    zero = jnp.zeros_like(block)
    return jnp.concatenate(
        [jnp.where(place < half, block, zero), jnp.where(place >= half, block, zero)],
        axis=1 - axis,
    )


def split_heads(source, stacked, pairs):
    block, base = source
    for p in range(pairs):
        for t in range(ROWS // KEYS):
            part = block[t * KEYS : (t + 1) * KEYS, p * 128 : (p + 1) * 128]
            stacked[p, base + t] = keep_pair(part, 1)


def split_heads_turned(source, stacked, pairs):
    block, base = source
    turned = block.T
    for p in range(pairs):
        for t in range(ROWS // KEYS):
            part = turned[p * 128 : (p + 1) * 128, t * KEYS : (t + 1) * KEYS]
            stacked[p, base + t] = keep_pair(part, 0)


def mask_bias(block_index, low, high):
    key_place = block_index * KEYS + iota((KEYS, ROWS), 0)
    return jnp.where((key_place >= low) & (key_place < high), 0.0, MASKED)


def attend_block(queries, keys, values_turned, span, mixed, top, total):
    low, high, least, most = span
    pairs = keys.shape[0]
    mixed[...] = jnp.zeros_like(mixed)
    top[...] = jnp.full(top.shape, MASKED, F32)
    total[...] = jnp.zeros_like(total)

    def one(j, carried):
        bias = mask_bias(j, low, high)
        for p in range(pairs):
            scores = mul_nt(keys[p, j], queries[:, p * 128 : (p + 1) * 128])
            weights, fades = [], []
            for u in range(2):
                h = 2 * p + u
                part = scores[u * KEYS : (u + 1) * KEYS] + bias
                old = top[h : h + 1, :]
                new = jnp.maximum(old, jnp.max(part, axis=0, keepdims=True))
                fade = jnp.exp(old - new)
                weight = jnp.exp(part - new)
                total[h : h + 1, :] = total[h : h + 1, :] * fade + jnp.sum(
                    weight, axis=0, keepdims=True
                )
                top[h : h + 1, :] = new
                weights.append(weight.astype(BF16))
                fades.append(fade)
            added = mul(values_turned[p, j], jnp.concatenate(weights, axis=0))
            for u in range(2):
                at = p * 128 + u * 64
                mixed[at : at + 64, :] = (
                    mixed[at : at + 64, :] * fades[u] + added[u * 64 : (u + 1) * 64]
                )
        return carried

    lax.fori_loop(least, most, one, 0)
    for h in range(2 * pairs):
        rate = 1.0 / total[h : h + 1, :]
        mixed[h * 64 : (h + 1) * 64, :] = mixed[h * 64 : (h + 1) * 64, :] * rate
    top[...] = top[...] + jnp.log(total[...])


def attend_block_back(
    queries, grads, keys, keys_turned, values, span, logs, inner, grad_queries, grad_keys, grad_values
):
    low, high, least, most = span
    pairs = keys.shape[0]
    grad_queries[...] = jnp.zeros_like(grad_queries)
    first_half = iota((KEYS, 128), 1) < 64

    def one(j, carried):
        bias = mask_bias(j, low, high)
        rows = pl.ds(pl.multiple_of(j * KEYS, KEYS), KEYS)
        for p in range(pairs):
            lanes = slice(p * 128, (p + 1) * 128)
            query = queries[:, lanes]
            grad = grads[:, lanes]
            scores = mul_nt(keys[p, j], query)
            grad_prob = mul_nt(values[p, j], grad)
            probs, grad_scores = [], []
            for u in range(2):
                h = 2 * p + u
                part = slice(u * KEYS, (u + 1) * KEYS)
                prob = jnp.exp(scores[part] + bias - logs[h : h + 1, :])
                probs.append(prob.astype(BF16))
                grad_scores.append((prob * (grad_prob[part] - inner[h : h + 1, :])).astype(BF16))
            prob_pair = jnp.concatenate(probs, axis=0)
            grad_pair = jnp.concatenate(grad_scores, axis=0)
            both = mul(prob_pair, grad)
            grad_values[rows, lanes] += jnp.where(first_half, both[:KEYS], both[KEYS:])
            both = mul(grad_pair, query)
            grad_keys[rows, lanes] += jnp.where(first_half, both[:KEYS], both[KEYS:])
            grad_queries[lanes, :] += mul(keys_turned[p, j], grad_pair)
        return carried

    lax.fori_loop(least, most, one, 0)


def row_inner(grads, mixed):
    width = grads.shape[1]
    head_of = iota((16, width), 1) // (width // HEADS)
    picks = (head_of == iota((16, width), 0)).astype(BF16)
    product = grads.astype(F32) * mixed.astype(F32)
    big = product.astype(BF16)
    small = (product - big.astype(F32)).astype(BF16)
    return mul_nt(picks, big) + mul_nt(picks, small)


def column(row):
    return jnp.broadcast_to(row, (128, row.shape[1])).T[:, :1]


class Copies:
    def __init__(self, sems):
        self.sems = sems
        self.used = 0

    def start(self, source, target):
        copy = pltpu.make_async_copy(source, target, self.sems.at[self.used])
        self.used += 1
        copy.start()
        return copy


def block_rows(i):
    return pl.ds(pl.multiple_of(i * ROWS, ROWS), ROWS)


def colsum(values):
    return jnp.sum(values, axis=0, keepdims=True)


def ffn_forward(low_in, base, weights):
    expand_w, expand_b, contract_w, contract_b = weights
    total = base + contract_b[...]
    for c in range(expand_w.shape[1] // PIECE):
        part = slice(c * PIECE, (c + 1) * PIECE)
        before = mul(low_in, expand_w[:, part]) + expand_b[:, part]
        total = total + mul(gate(before).astype(BF16), contract_w[part, :])
    return total


def ffn_forward_kept(low_in, base, weights, hidden, slopes):
    expand_w, expand_b, contract_w, contract_b = weights
    total = base + contract_b[...]
    for c in range(expand_w.shape[1] // PIECE):
        part = slice(c * PIECE, (c + 1) * PIECE)
        before = mul(low_in, expand_w[:, part]) + expand_b[:, part]
        gated, slope = gate_and_slope(before)
        gated = gated.astype(BF16)
        hidden(part, gated)
        slopes[:, part] = slope
        total = total + mul(gated, contract_w[part, :])
    return total


def ffn_back(grad_summed, weights, slopes, grad_before, small):
    expand_w, _, contract_w, _ = weights
    branch = grad_summed.astype(BF16)
    grad_in = grad_summed
    for c in range(expand_w.shape[1] // PIECE):
        part = slice(c * PIECE, (c + 1) * PIECE)
        pushed = (mul_nt(branch, contract_w[part, :]) * slopes[:, part]).astype(BF16)
        grad_before(part, pushed)
        small[8 + c : 9 + c, :] += colsum(pushed.astype(F32))
        grad_in = grad_in + mul_nt(pushed, expand_w[:, part])
    return branch, grad_in


def first_kernel(
    side_ref, lengths, tokens, halting, weight_in, weight_out, expand_w, expand_b, contract_w,
    contract_b, cross_w, value_w, gains, shifts,
    start_low, projected, attended, logs, first_sum, memory, memory_low,
    tok, win, wout, w1, w2, table_big, table_small, start, proj, keys, values_turned, mixed, top, total,
    att, fsum, mem, meml, slow, sems,
):
    side = side_ref[0]
    blocks = tokens.shape[0] // ROWS
    width = tokens.shape[1]
    pairs = width // 128
    cp = Copies(sems)
    c_tok = cp.start(tokens, tok)
    c_in = cp.start(weight_in, win)
    c_out = cp.start(weight_out, wout)
    c_w1 = cp.start(expand_w, w1)
    c_w2 = cp.start(contract_w, w2)

    half = width // 2
    rate = jnp.exp(iota((16, half), 1).astype(F32) * (-math.log(10000.0) / half))
    fine = iota((16, half), 0).astype(F32) * rate
    coarse = fine * 16.0
    fine_s, fine_c, coarse_s, coarse_c = jnp.sin(fine), jnp.cos(fine), jnp.sin(coarse), jnp.cos(coarse)
    step_s, step_c = fine_s[STEP : STEP + 1], fine_c[STEP : STEP + 1]
    for a in range(LONGEST // 16):
        s, c = coarse_s[a : a + 1], coarse_c[a : a + 1]
        whole = jnp.concatenate(
            [s * fine_c + c * fine_s + step_s, c * fine_c - s * fine_s + step_c], axis=1
        )
        big = whole.astype(BF16)
        table_big[a * 16 : (a + 1) * 16, :] = big
        table_small[a * 16 : (a + 1) * 16, :] = (whole - big.astype(F32)).astype(BF16)

    lane = iota((1, 128), 1)
    begins = jnp.zeros((1, 128), jnp.int32)
    at = jnp.int32(0)
    for k in range(lengths.shape[1]):
        begins = jnp.where(lane == k, at, begins)
        at = at + lengths[side, k]
    c_tok.wait()
    c_in.wait()

    def prepare(i, carried):
        rows = block_rows(i)
        place = i * ROWS + iota((ROWS, 1), 0)
        began = jnp.max(jnp.where(place >= begins, begins, 0), axis=1, keepdims=True)
        picks = (iota((ROWS, LONGEST), 1) == place - began).astype(F32).astype(BF16)
        block = tok[rows, :].astype(F32) + (mul(picks, table_big[...]) + mul(picks, table_small[...]))
        start[rows, :] = block
        low = block.astype(BF16)
        slow[rows, :] = low
        sent = mul(low, win[...]).astype(BF16)
        proj[rows, :] = sent
        split_heads((sent[:, width : 2 * width], 2 * i), keys, pairs)
        split_heads_turned((sent[:, 2 * width :], 2 * i), values_turned, pairs)
        return carried

    lax.fori_loop(0, blocks, prepare, 0)
    c_slow = cp.start(slow, start_low)
    c_proj = cp.start(proj, projected)
    c_out.wait()
    c_w1.wait()
    c_w2.wait()
    weights = (w1, expand_b, w2, contract_b)

    def attend(i, carried):
        rows = block_rows(i)
        queries = proj[rows, :width] * BF16(1.0 / math.sqrt(width // HEADS))
        attend_block(
            queries, keys, values_turned, bounds(lengths, side, side, i, side == 1), mixed, top, total
        )
        logs[i] = top[...]
        low = mixed[...].astype(BF16).T
        att[rows, :] = low
        summed = start[rows, :] + mul(low, wout[...])
        fsum[rows, :] = summed

        @pl.when(side == 0)
        def _():
            first = norm_parts(summed)[0] * gains[0:1, :] + shifts[0:1, :]
            tail = norm_parts(ffn_forward(first.astype(BF16), first, weights))[0] * gains[1:2, :] + shifts[1:2, :]
            state = tok[rows, :].astype(F32)
            running = column(halting[:, block_rows(i)].astype(F32))
            stepped = state + running * (tail - state)
            kept = norm_parts(stepped)[0] * gains[2:3, :] + shifts[2:3, :]
            mem[rows, :] = kept
            meml[rows, :] = kept.astype(BF16)

        return carried

    lax.fori_loop(0, blocks, attend, 0)
    c_att = cp.start(att, attended)
    c_fsum = cp.start(fsum, first_sum)

    @pl.when(side == 0)
    def _():
        a = cp.start(mem, memory)
        b = cp.start(meml, memory_low)
        a.wait()
        b.wait()

    for c in (c_slow, c_proj, c_att, c_fsum):
        c.wait()


ANY = pl.BlockSpec(memory_space=pl.ANY)
SMEM = pl.BlockSpec(memory_space=pltpu.SMEM)
VMEM = pl.BlockSpec(memory_space=pltpu.VMEM)


def shape(s, d):
    return jax.ShapeDtypeStruct(s, d)


def call(kernel, ins, outs, scratch, flops, moved, aliases=None, name=None):
    return pl.pallas_call(
        kernel,
        in_specs=ins,
        out_specs=[o[1] for o in outs],
        out_shape=[o[0] for o in outs],
        scratch_shapes=scratch,
        input_output_aliases=aliases or {},
        compiler_params=pltpu.CompilerParams(vmem_limit_bytes=VMEM_BYTES),
        cost_estimate=pl.CostEstimate(flops=flops, bytes_accessed=moved, transcendentals=0),
        name=name,
    )


def run_first(side, lengths, tokens, halting, weight_in, weight_out, expand_w, expand_b, contract_w, contract_b, cross_w, value_w, gains, shifts):
    n, d = tokens.shape
    ff = expand_w.shape[1]
    pairs, nk = d // 128, n // KEYS
    V = pltpu.VMEM
    return call(
        first_kernel,
        [SMEM, SMEM, ANY, VMEM, ANY, ANY, ANY, VMEM, ANY, VMEM, ANY, ANY, VMEM, VMEM],
        [
            (shape((n, d), BF16), ANY),
            (shape((n, 3 * d), BF16), ANY),
            (shape((n, d), BF16), ANY),
            (shape((n // ROWS, HEADS, ROWS), F32), VMEM),
            (shape((n, d), F32), ANY),
            (shape((n, d), F32), ANY),
            (shape((n, d), BF16), ANY),
        ],
        [
            V((n, d), BF16), V((d, 3 * d), BF16), V((d, d), BF16), V((d, ff), BF16), V((ff, d), BF16),
            V((LONGEST, d), BF16), V((LONGEST, d), BF16), V((n, d), F32), V((n, 3 * d), BF16),
            V((pairs, nk, 2 * KEYS, 128), BF16), V((pairs, nk, 128, 2 * KEYS), BF16),
            V((d, ROWS), F32), V((HEADS, ROWS), F32), V((HEADS, ROWS), F32),
            V((n, d), BF16), V((n, d), F32), V((n, d), F32), V((n, d), BF16), V((n, d), BF16),
            pltpu.SemaphoreType.DMA((11,)),
        ],
        12_000_000_000, 20_000_000, name="first_part",
    )(side, lengths, tokens, halting, weight_in, weight_out, expand_w, expand_b, contract_w, contract_b, cross_w, value_w, gains, shifts)


SMALL_ROWS = 16


def middle_kernel(
    side_ref, lengths, tokens, halting, cotangent, first_sum, memory_in, key_w, value_w, cross_w, mix_w,
    expand_w, expand_b, contract_w, contract_b, gains, shifts, memory,
    result, hidden, branch, grad_before, ffn_in, grad_first, grad_memory,
    pairs_low, crossed, grad_cross, first_low, grad_query, small,
    mlow, kw, vw, cw, mw, w1, w2, tok, cot, fsum, keys, keys_t, values, values_t, slopes,
    mixed, top, total, gqt, gk, gv, res, hid, bra, gbef, fin, gfirst, gmem, plow, cro, gcro, flow, gqry, sems,
):
    side = side_ref[0]
    n, width = tok.shape
    blocks = n // ROWS
    pairs = width // 128
    scale = 1.0 / math.sqrt(width // HEADS)

    @pl.when(side == 1)
    def _():
        cp = Copies(sems)
        c_mlow = cp.start(memory_in, mlow)
        c_kw, c_vw = cp.start(key_w, kw), cp.start(value_w, vw)
        rest = [
            cp.start(a, b)
            for a, b in (
                (cross_w, cw), (mix_w, mw), (first_sum, fsum), (expand_w, w1), (contract_w, w2),
                (tokens, tok), (cotangent, cot),
            )
        ]
        small[...] = jnp.zeros_like(small)
        gk[...] = jnp.zeros_like(gk)
        gv[...] = jnp.zeros_like(gv)
        c_mlow.wait()
        c_kw.wait()
        c_vw.wait()

        def prepare(i, carried):
            low = mlow[block_rows(i), :]
            key = mul(low, kw[...]).astype(BF16)
            value = mul(low, vw[...]).astype(BF16)
            split_heads((key, 2 * i), keys, pairs)
            split_heads((value, 2 * i), values, pairs)
            split_heads_turned((key, 2 * i), keys_t, pairs)
            split_heads_turned((value, 2 * i), values_t, pairs)
            return carried

        lax.fori_loop(0, blocks, prepare, 0)
        for c in rest:
            c.wait()
        weights = (w1, expand_b, w2, contract_b)

        def one(i, carried):
            rows = block_rows(i)
            first = norm_parts(fsum[rows, :])[0] * gains[0:1, :] + shifts[0:1, :]
            low = first.astype(BF16)
            flow[rows, :] = low
            queries = mul(low, cw[...]).astype(BF16) * BF16(scale)
            span = bounds(lengths, 1, 0, i, None)
            attend_block(queries, keys, values_t, span, mixed, top, total)
            mix_low = mixed[...].astype(BF16).T
            cro[rows, :] = mix_low
            unit2, rate2 = norm_parts(first + mul(mix_low, mw[...]))
            second = unit2 * gains[2:3, :] + shifts[2:3, :]
            low = second.astype(BF16)
            fin[rows, :] = low

            def keep_hidden(part, value):
                hid[rows, part] = value

            def keep_before(part, value):
                gbef[rows, part] = value

            unit1, rate1 = norm_parts(ffn_forward_kept(low, second, weights, keep_hidden, slopes))
            state = tok[rows, :].astype(F32)
            running = column(halting[:, block_rows(i)].astype(F32))
            res[rows, :] = state + running * (unit1 * gains[1:2, :] + shifts[1:2, :] - state)
            grad = running * cot[rows, :]
            small[1:2, :] += colsum(grad * unit1)
            small[4:5, :] += colsum(grad)
            grad_low, grad = ffn_back(
                norm_back(grad, unit1, rate1, gains[1:2, :]), weights, slopes, keep_before, small
            )
            bra[rows, :] = grad_low
            small[6:7, :] += colsum(grad_low.astype(F32))
            small[2:3, :] += colsum(grad * unit2)
            small[5:6, :] += colsum(grad)
            grad = norm_back(grad, unit2, rate2, gains[2:3, :])
            grad_low = grad.astype(BF16)
            gcro[rows, :] = grad_low
            grad_mix = mul_nt(grad_low, mw[...]).astype(BF16)
            attend_block_back(
                queries, grad_mix, keys, keys_t, values, span, top, row_inner(grad_mix, mix_low), gqt, gk, gv
            )
            grad_low = (gqt[...] * scale).astype(BF16).T
            gqry[rows, :] = grad_low
            gfirst[rows, :] = grad + mul_nt(grad_low, cw[...])
            return carried

        lax.fori_loop(0, blocks, one, 0)

        def finish(i, carried):
            rows = block_rows(i)
            key = gk[rows, :].astype(BF16)
            value = gv[rows, :].astype(BF16)
            plow[rows, :width] = key
            plow[rows, width:] = value
            gmem[rows, :] = (mul_nt(key, kw[...]) + mul_nt(value, vw[...])).astype(BF16)
            return carried

        lax.fori_loop(0, blocks, finish, 0)
        outs = [
            cp.start(a, b)
            for a, b in (
                (gmem, grad_memory), (res, result), (hid, hidden), (bra, branch), (gbef, grad_before),
                (fin, ffn_in), (gfirst, grad_first), (plow, pairs_low), (cro, crossed), (gcro, grad_cross),
                (flow, first_low), (gqry, grad_query),
            )
        ]
        for c in outs:
            c.wait()


def run_middle(side, lengths, tokens, halting, cotangent, first_sum, memory_in, key_w, value_w, cross_w, mix_w, expand_w, expand_b, contract_w, contract_b, gains, shifts, memory):
    n, d = tokens.shape
    ff = expand_w.shape[1]
    pairs, nk = d // 128, n // KEYS
    V = pltpu.VMEM
    return call(
        middle_kernel,
        [SMEM, SMEM, ANY, VMEM, ANY, ANY, ANY, ANY, ANY, ANY, ANY, ANY, VMEM, ANY, VMEM, VMEM, VMEM, ANY],
        [
            (shape((n, d), F32), ANY),
            (shape((n, ff), BF16), ANY),
            (shape((n, d), BF16), ANY),
            (shape((n, ff), BF16), ANY),
            (shape((n, d), BF16), ANY),
            (shape((n, d), F32), ANY),
            (shape((n, d), BF16), ANY),
            (shape((n, 2 * d), BF16), ANY),
            (shape((n, d), BF16), ANY),
            (shape((n, d), BF16), ANY),
            (shape((n, d), BF16), ANY),
            (shape((n, d), BF16), ANY),
            (shape((SMALL_ROWS, d), F32), VMEM),
        ],
        [
            V((n, d), BF16), V((d, d), BF16), V((d, d), BF16), V((d, d), BF16), V((d, d), BF16),
            V((d, ff), BF16), V((ff, d), BF16), V((n, d), BF16), V((n, d), F32), V((n, d), F32),
            V((pairs, nk, 2 * KEYS, 128), BF16), V((pairs, nk, 128, 2 * KEYS), BF16),
            V((pairs, nk, 2 * KEYS, 128), BF16), V((pairs, nk, 128, 2 * KEYS), BF16),
            V((ROWS, ff), F32), V((d, ROWS), F32), V((HEADS, ROWS), F32), V((HEADS, ROWS), F32), V((d, ROWS), F32),
            V((n, d), F32), V((n, d), F32), V((n, d), F32), V((n, ff), BF16), V((n, d), BF16), V((n, ff), BF16),
            V((n, d), BF16), V((n, d), F32), V((n, d), BF16), V((n, 2 * d), BF16), V((n, d), BF16),
            V((n, d), BF16), V((n, d), BF16), V((n, d), BF16),
            pltpu.SemaphoreType.DMA((24,)),
        ],
        24_000_000_000, 40_000_000, aliases={17: 0}, name="target_middle",
    )(side, lengths, tokens, halting, cotangent, first_sum, memory_in, key_w, value_w, cross_w, mix_w, expand_w, expand_b, contract_w, contract_b, gains, shifts, memory)


def source_back_kernel(
    side_ref, tokens, halting, cotangent, first_sum, grad_memory,
    expand_w, expand_b, contract_w, contract_b, gains, shifts,
    hidden_in, branch_in, before_in, ffn_in_in, first_in, small_in,
    hidden, branch, grad_before, ffn_in, grad_first, small, grad_direct,
    gmem, w1, w2, tok, cot, fsum, slopes, hid, bra, gbef, fin, gfirst, gdir, sems,
):
    side = side_ref[0]
    n, width = tok.shape
    blocks = n // ROWS

    small[...] = small_in[...]

    @pl.when(side == 0)
    def _():
        cp = Copies(sems)
        ins = [
            cp.start(a, b)
            for a, b in (
                (first_sum, fsum), (expand_w, w1), (contract_w, w2), (tokens, tok), (cotangent, cot),
                (grad_memory, gmem),
            )
        ]
        small[...] = jnp.zeros_like(small)
        for c in ins:
            c.wait()
        weights = (w1, expand_b, w2, contract_b)

        def one(i, carried):
            rows = block_rows(i)
            first = norm_parts(fsum[rows, :])[0] * gains[0:1, :] + shifts[0:1, :]
            low = first.astype(BF16)
            fin[rows, :] = low

            def keep_hidden(part, value):
                hid[rows, part] = value

            def keep_before(part, value):
                gbef[rows, part] = value

            unit1, rate1 = norm_parts(ffn_forward_kept(low, first, weights, keep_hidden, slopes))
            state = tok[rows, :].astype(F32)
            running = column(halting[:, block_rows(i)].astype(F32))
            unit2, rate2 = norm_parts(
                state + running * (unit1 * gains[1:2, :] + shifts[1:2, :] - state)
            )
            grad = cot[rows, :] + gmem[rows, :].astype(F32)
            small[2:3, :] += colsum(grad * unit2)
            small[5:6, :] += colsum(grad)
            grad = norm_back(grad, unit2, rate2, gains[2:3, :])
            gdir[rows, :] = (1.0 - running) * grad
            grad = running * grad
            small[1:2, :] += colsum(grad * unit1)
            small[4:5, :] += colsum(grad)
            grad_low, grad = ffn_back(
                norm_back(grad, unit1, rate1, gains[1:2, :]), weights, slopes, keep_before, small
            )
            bra[rows, :] = grad_low
            small[6:7, :] += colsum(grad_low.astype(F32))
            gfirst[rows, :] = grad
            return carried

        lax.fori_loop(0, blocks, one, 0)
        outs = [
            cp.start(a, b)
            for a, b in (
                (hid, hidden), (bra, branch), (gbef, grad_before), (fin, ffn_in), (gfirst, grad_first),
                (gdir, grad_direct),
            )
        ]
        for c in outs:
            c.wait()


def run_source_back(side, tokens, halting, cotangent, first_sum, grad_memory, expand_w, expand_b, contract_w, contract_b, gains, shifts, hidden, branch, before, ffn_in, first, small):
    n, d = tokens.shape
    ff = expand_w.shape[1]
    V = pltpu.VMEM
    return call(
        source_back_kernel,
        [SMEM, ANY, VMEM, ANY, ANY, ANY, ANY, VMEM, ANY, VMEM, VMEM, VMEM, ANY, ANY, ANY, ANY, ANY, VMEM],
        [
            (shape((n, ff), BF16), ANY), (shape((n, d), BF16), ANY), (shape((n, ff), BF16), ANY),
            (shape((n, d), BF16), ANY), (shape((n, d), F32), ANY), (shape((SMALL_ROWS, d), F32), VMEM),
            (shape((n, d), F32), ANY),
        ],
        [
            V((n, d), BF16), V((d, ff), BF16), V((ff, d), BF16), V((n, d), BF16), V((n, d), F32), V((n, d), F32),
            V((ROWS, ff), F32), V((n, ff), BF16), V((n, d), BF16), V((n, ff), BF16), V((n, d), BF16),
            V((n, d), F32), V((n, d), F32), pltpu.SemaphoreType.DMA((12,)),
        ],
        13_000_000_000, 30_000_000, aliases={12: 0, 13: 1, 14: 2, 15: 3, 16: 4, 17: 5}, name="source_back",
    )(side, tokens, halting, cotangent, first_sum, grad_memory, expand_w, expand_b, contract_w, contract_b, gains, shifts, hidden, branch, before, ffn_in, first, small)


def self_back_kernel(
    side_ref, lengths, halting, cotangent, first_sum, grad_first, grad_direct, projected, attended, logs,
    weight_in, weight_out, gains,
    input_grad, grad_projected, grad_mix, small,
    cot, fsum, gfirst, gdir, proj, att, win, wout, keys, keys_t, values, gqt, gk, gv, gsum, gmix, gproj, ingrad, sems,
):
    side = side_ref[0]
    n, width = cot.shape
    blocks = n // ROWS
    pairs = width // 128
    scale = 1.0 / math.sqrt(width // HEADS)
    cp = Copies(sems)
    c_proj = cp.start(projected, proj)
    ins = [
        cp.start(a, b)
        for a, b in (
            (first_sum, fsum), (grad_first, gfirst), (weight_out, wout), (attended, att),
            (cotangent, cot), (grad_direct, gdir), (weight_in, win),
        )
    ]
    small[...] = jnp.zeros_like(small)
    gk[...] = jnp.zeros_like(gk)
    gv[...] = jnp.zeros_like(gv)
    c_proj.wait()

    def prepare(i, carried):
        rows = block_rows(i)
        split_heads((proj[rows, width : 2 * width], 2 * i), keys, pairs)
        split_heads_turned((proj[rows, width : 2 * width], 2 * i), keys_t, pairs)
        split_heads((proj[rows, 2 * width :], 2 * i), values, pairs)
        return carried

    lax.fori_loop(0, blocks, prepare, 0)
    for c in ins:
        c.wait()

    def one(i, carried):
        rows = block_rows(i)
        unit, rate = norm_parts(fsum[rows, :])
        grad = gfirst[rows, :]
        small[0:1, :] += colsum(grad * unit)
        small[3:4, :] += colsum(grad)
        grad = norm_back(grad, unit, rate, gains[0:1, :])
        gsum[rows, :] = grad
        grad_low = grad.astype(BF16)
        gmix[rows, :] = grad_low
        grad_att = mul_nt(grad_low, wout[...]).astype(BF16)
        queries = proj[rows, :width] * BF16(scale)
        span = bounds(lengths, side, side, i, side == 1)
        attend_block_back(
            queries, grad_att, keys, keys_t, values, span, logs[i], row_inner(grad_att, att[rows, :]), gqt, gk, gv
        )
        gproj[rows, :width] = (gqt[...] * scale).astype(BF16).T
        return carried

    lax.fori_loop(0, blocks, one, 0)

    def finish(i, carried):
        rows = block_rows(i)
        gproj[rows, width : 2 * width] = gk[rows, :].astype(BF16)
        gproj[rows, 2 * width :] = gv[rows, :].astype(BF16)
        ingrad[rows, :] = gsum[rows, :] + mul_nt(gproj[rows, :], win[...])

        @pl.when(side == 0)
        def _():
            ingrad[rows, :] += gdir[rows, :]

        @pl.when(side == 1)
        def _():
            running = column(halting[:, block_rows(i)].astype(F32))
            ingrad[rows, :] += (1.0 - running) * cot[rows, :]

        return carried

    lax.fori_loop(0, blocks, finish, 0)
    outs = [
        cp.start(a, b) for a, b in ((ingrad, input_grad), (gproj, grad_projected), (gmix, grad_mix))
    ]
    for c in outs:
        c.wait()


def run_self_back(side, lengths, halting, cotangent, first_sum, grad_first, grad_direct, projected, attended, logs, weight_in, weight_out, gains):
    n, d = cotangent.shape
    pairs, nk = d // 128, n // KEYS
    V = pltpu.VMEM
    return call(
        self_back_kernel,
        [SMEM, SMEM, VMEM, ANY, ANY, ANY, ANY, ANY, ANY, VMEM, ANY, ANY, VMEM],
        [
            (shape((n, d), F32), ANY), (shape((n, 3 * d), BF16), ANY), (shape((n, d), BF16), ANY),
            (shape((SMALL_ROWS, d), F32), VMEM),
        ],
        [
            V((n, d), F32), V((n, d), F32), V((n, d), F32), V((n, d), F32), V((n, 3 * d), BF16), V((n, d), BF16),
            V((d, 3 * d), BF16), V((d, d), BF16),
            V((pairs, nk, 2 * KEYS, 128), BF16), V((pairs, nk, 128, 2 * KEYS), BF16), V((pairs, nk, 2 * KEYS, 128), BF16),
            V((d, ROWS), F32), V((n, d), F32), V((n, d), F32), V((n, d), F32), V((n, d), BF16), V((n, 3 * d), BF16),
            V((n, d), F32), pltpu.SemaphoreType.DMA((12,)),
        ],
        16_000_000_000, 30_000_000, name="self_back",
    )(side, lengths, halting, cotangent, first_sum, grad_first, grad_direct, projected, attended, logs, weight_in, weight_out, gains)


def exchange(mine, bit, axis):
    count = lax.axis_size(axis)
    return lax.ppermute(mine, axis, [(i, i ^ bit) for i in range(count)])


def take(parts, index):
    return lax.dynamic_index_in_dim(parts, index, 0, keepdims=False)


def halve(value, bit, axis):
    own = (lax.axis_index(axis) // bit) % 2
    parts = value.reshape((2, value.shape[0] // 2) + value.shape[1:])
    came = exchange(take(parts, 1 - own), bit, axis)
    return (take(parts, own).astype(F32) + came.astype(F32)).astype(BF16)


def double(value, bit, axis):
    own = (lax.axis_index(axis) // bit) % 2
    came = exchange(value, bit, axis)
    low = jnp.where(own == 0, value, came)
    high = jnp.where(own == 0, came, value)
    return jnp.concatenate([low, high], axis=0)


def sum_over(value, axis):
    bits = []
    bit = 1
    while bit < lax.axis_size(axis):
        bits.append(bit)
        bit *= 2
    for bit in bits:
        value = halve(value, bit, axis)
    for bit in reversed(bits):
        value = double(value, bit, axis)
    return value


def mul_tn(left, right):
    return lax.dot_general(left, right, (((0,), (0,)), ((), ())), preferred_element_type=F32)


def body(
    tokens, cotangent, lengths, halting, attention_in, attention_out, cross_first, cross_second,
    expand_weight, expand_bias, contract_weight, contract_bias, norm_gain, norm_bias,
):
    side_index = lax.axis_index("half")
    side = side_index.astype(jnp.int32).reshape((1,))
    tok, cot = tokens[0, 0], cotangent[0, 0]
    lens = lengths[:, 0]
    halt = halting[0]
    w_in, w_out, w_one, w_two = attention_in[0], attention_out[0], cross_first[0], cross_second[0]
    w1, w2 = expand_weight[0], contract_weight[0]
    gains, shifts = norm_gain[0], norm_bias[0]
    n, d = tok.shape
    ff = w1.shape[1]
    there, back = [(0, 1)], [(1, 0)]
    source_pair = lax.ppermute(jnp.concatenate([w_one, w_two], axis=0), "half", there)
    start_low, projected, attended, logs, first_sum, memory, memory_low = run_first(
        side, lens, tok, halt, w_in, w_out, w1, expand_bias, w2, contract_bias, w_one, w_two, gains, shifts
    )
    memory_in = lax.ppermute(memory_low, "half", there)
    (
        result, hidden, branch, grad_before, ffn_in, grad_first, grad_memory,
        pairs_low, crossed, grad_cross, first_low, grad_query, small_one,
    ) = run_middle(
        side, lens, tok, halt, cot, first_sum, memory_in, source_pair[:d], source_pair[d:], w_one, w_two,
        w1, expand_bias, w2, contract_bias, gains, shifts, memory,
    )
    grad_in = lax.ppermute(grad_memory, "half", back)
    hidden, branch, grad_before, ffn_in, grad_first, small_one, grad_direct = run_source_back(
        side, tok, halt, cot, first_sum, grad_in, w1, expand_bias, w2, contract_bias, gains, shifts,
        hidden, branch, grad_before, ffn_in, grad_first, small_one,
    )

    def cross_grads():
        return jnp.concatenate(
            [
                mul_tn(first_low, grad_query).astype(BF16),
                mul_tn(crossed, grad_cross).astype(BF16),
                mul_tn(memory_in, pairs_low[:, :d]).astype(BF16),
                mul_tn(memory_in, pairs_low[:, d:]).astype(BF16),
            ],
            axis=0,
        )

    cross = lax.cond(side_index == 1, cross_grads, lambda: jnp.zeros((4 * d, d), BF16))
    ffn = jnp.concatenate(
        [mul_tn(hidden, branch).astype(BF16), mul_tn(grad_before, ffn_in).astype(BF16)], axis=0
    )
    input_grad, grad_projected, grad_mix, small_two = run_self_back(
        side, lens, halt, cot, first_sum, grad_first, grad_direct, projected, attended, logs, w_in, w_out, gains
    )
    attn = jnp.concatenate(
        [
            mul_tn(grad_projected, start_low).astype(BF16),
            mul_tn(attended, grad_mix).astype(BF16),
            (small_one + small_two).astype(BF16),
        ],
        axis=0,
    )
    attn = jnp.concatenate([attn, jnp.zeros((-attn.shape[0] % 1024, d), BF16)], axis=0)
    cross = sum_over(cross, "dp")
    ffn = sum_over(ffn, "dp")
    attn = sum_over(attn, "dp")
    from_target = lax.ppermute(cross[2 * d :], "half", back)
    cross = jnp.where(side_index == 1, cross[: 2 * d], from_target).astype(F32)
    small = attn[4 * d : 4 * d + SMALL_ROWS].astype(F32)
    return (
        result[None, None],
        input_grad[None, None],
        attn[: 3 * d].astype(F32).T[None],
        attn[3 * d : 4 * d].astype(F32)[None],
        cross[:d][None],
        cross[d:][None],
        ffn[ff:].astype(F32).T[None],
        small[8 : 8 + ff // d].reshape(1, ff),
        ffn[:ff].astype(F32)[None],
        small[6:7],
        small[0:3][None],
        small[3:6][None],
    )


def solution(mesh):
    placed = (
        P("half", "dp", None, None),
        P("half", "dp", None, None),
        P(None, "dp", None),
        P("half", "dp", None),
        P("half", None, None),
        P("half", None, None),
        P("half", None, None),
        P("half", None, None),
        P("half", None, None),
        P("half", None),
        P("half", None, None),
        P("half", None),
        P("half", None, None),
        P("half", None, None),
    )
    return jax.shard_map(
        body,
        mesh=mesh,
        in_specs=placed,
        out_specs=(
            P("half", "dp", None, None),
            P("half", "dp", None, None),
            P("half", None, None),
            P("half", None, None),
            P("half", None, None),
            P("half", None, None),
            P("half", None, None),
            P("half", None),
            P("half", None, None),
            P("half", None),
            P("half", None, None),
            P("half", None, None),
        ),
        check_vma=False,
    )
```

time: 970 us -> 468 us (0.48)
  waiting for transfers between devices: 494 us -> 271 us
  matrix products: 170 us -> 8.69 us
  Pallas kernels: 0 us -> 105 us
  local copies, waits for them, and re-layouts: 115 us -> 22.9 us
  blocking collectives: 64 us -> 0 us
  other arithmetic: 89.2 us -> 39.6 us
  between operations: 15.1 us -> 1.62 us
  starting transfers between devices: 3.92 us -> 16 us
  loops' own time: 11.6 us -> 0.02 us
    psum x1 -> x0, waiting for transfers between devices: 192 us -> none  [body(): lax.psum((grad_weight_in, grad_weight_mix, grad_gain_zero, grad_shift_zer...]
    dot_general x33 -> x4, matrix products: 170 us -> 8.69 us  [mul_tn(): lax.dot_general(left, right, (((0,), (0,)), ((), ())), preferred_element_...]
    pallas_call x0 -> x4, Pallas kernels: none -> 105 us  [the longest x1 41 us: run_first(): call(first_kernel, [SMEM, SMEM, ANY, VMEM, ANY, ANY, ANY, VMEM, ANY, VMEM...]
    psum x1 -> x0, blocking collectives: 64 us -> none  [body(): lax.psum((grad_weight_in, grad_weight_mix, grad_gain_zero, grad_shift_zer...]
    ppermute x2 -> x28, waiting for transfers between devices: 301 us -> 271 us  [the longest x24 152 us: exchange(): return lax.ppermute(mine, axis, [(i, i ^ bit) for i in range(count)])]
    reduce_sum x17 -> x0, other arithmetic: 27.7 us -> none  [the longest x5 8.83 us: layer_norm(): center = summed - jnp.mean(summed, axis=-1, keepdims=True)]
    cond x31 -> x0, local copies, waits for them, and re-layouts: 22.9 us -> none  [the longest x3 11.2 us: body(): lax.cond(encoding, encode_back, keep_decoded, (after_self, grad_arrived,...]
    unnamed x150 -> x47, local copies, waits for them, and re-layouts: 27 us -> 7.01 us
  transfers between devices with their start and end apart: 3 -> 28, of which waited for: 3 -> 19; matrix products, arithmetic and copies ran while one was open for 1% -> 11% of each run, Pallas kernels for 0% -> 22%
where the time goes in v1:
time: 468 us; the launch traced here: 465 us
  waiting for transfers between devices  271 us (58%)
  Pallas kernels  105 us (22%)
  other arithmetic  39.6 us (8%)
  local copies, waits for them, and re-layouts  22.9 us (5%)
  starting transfers between devices  16 us (3%)
  matrix products  8.69 us (2%)
    ppermute x24, waiting for transfers between devices, exchange(): return lax.ppermute(mine, axis, [(i, i ^ bit) for i in range(count)])  152 us
    ppermute x1, waiting for transfers between devices, body(): grad_in = lax.ppermute(grad_memory, 'half', back)  97.8 us
    pallas_call x1, Pallas kernels, run_first(): call(first_kernel, [SMEM, SMEM, ANY, VMEM, ANY, ANY, ANY, VMEM, ANY, VMEM...  41 us
    pallas_call x1, Pallas kernels, run_self_back(): call(self_back_kernel, [SMEM, SMEM, VMEM, ANY, ANY, ANY, ANY, ANY, ANY, V...  34.5 us
    pallas_call x1, Pallas kernels, run_source_back(): call(source_back_kernel, [SMEM, ANY, VMEM, ANY, ANY, ANY, ANY, VMEM, ANY,...  27.5 us
    ppermute x1, waiting for transfers between devices, body(): memory_in = lax.ppermute(memory_low, 'half', there)  21.6 us
    convert_element_type x12, other arithmetic, halve(): return (take(parts, own).astype(F32) + came.astype(F32)).astype(BF16)  11.1 us
  transfers between devices with their start and end apart: 28, of which 19 were waited for; matrix products, arithmetic and copies ran while one was open for 11% of the time, Pallas kernels for 22%

profile of v1, /device:TPU:0, one launch (start us, length us, event | category | flops | bytes accessed | tf_op | source)
XLA Modules:
  0.0 464.7 jit_solution(2641205565318511704)
XLA Ops:
  2.0 4.9 %collective-permute-start.1 = (bf16[1024,512]{1,0:T(8,128)(2,1)S(1)}, bf16[1024,512]{1,0:T(8,128)(2,1)S(1)}, u32[]{:S(2)}, u32[]{:S(2)}) collective-permute-start(bf16[1024,512]{1,0:T(8,128)(2,1)S(1)} %pad_maximum_fusion.4), channel_id=1, source_target_pairs={{0,16},{1,17},{2,18},{3,19},{4,20},{5,21},{6,22},{7,23},{8,24},{9,... | collective-permute-start | bytes 3145736 | tf_op jit(solution)/shard_map/ppermute | solution.py:844
  7.5 41.0 %first_part.1 = (bf16[1024,512]{1,0:T(8,128)(2,1)}, bf16[1024,1536]{1,0:T(8,128)(2,1)}, bf16[1024,512]{1,0:T(8,128)(2,1)}, f32[4,8,256]{2,1,0:T(8,128)}, f32[102...) custom-call(s32[1]{0:T(128)} %bitcast.1.side_ref, s32[2,16]{1,0:T(2,128)} %bitcast.181, ...), custom_call_target="tpu_custom_call" | custom-call | flops 12000000000 | bytes 20000000 | tf_op jit(solution)/shard_map/first_part/pallas_call | solution.py:405
  51.0 21.6 %collective-permute-done.memory_in = bf16[1024,512]{1,0:T(8,128)(2,1)S(1)} collective-permute-done((bf16[1024,512]{1,0:T(8,128)(2,1)}, bf16[1024,512]{1,0:T(8,128)(2,1)S(1)}, u32[]{:S(2)}, u32[]{:S(2)}) %collective-permute-start) | collective-permute-done | bytes 1048608 | tf_op jit(solution)/shard_map/ppermute | solution.py:848
  80.9 97.8 %collective-permute-done.2.grad_memory = bf16[1024,512]{1,0:T(8,128)(2,1)} collective-permute-done((bf16[1024,512]{1,0:T(8,128)(2,1)}, bf16[1024,512]{1,0:T(8,128)(2,1)}, u32[]{:S(2)}, u32[]{:S(2)}) %collective-permute-start.2) | collective-permute-done | bytes 1048608 | tf_op jit(solution)/shard_map/ppermute | solution.py:856
  178.6 27.5 %source_back.1 = (bf16[1024,2048]{1,0:T(8,128)(2,1)}, bf16[1024,512]{1,0:T(8,128)(2,1)}, bf16[1024,2048]{1,0:T(8,128)(2,1)}, bf16[1024,512]{1,0:T(8,128)(2,1)}, ...) custom-call(s32[1]{0:T(128)} %bitcast.1.side_ref, ...), custom_call_target="tpu_custom_call", output_to_operand_aliasing={{0}: (12, {}), {1}: (13, {}), {2}: (14, {}), {3}: (15, {}),... | custom-call | flops 12999999488 | bytes 30000000 | tf_op jit(solution)/shard_map/source_back/pallas_call | solution.py:667
  206.1 34.5 %self_back.1 = (f32[1024,512]{1,0:T(8,128)}, bf16[1024,1536]{1,0:T(8,128)(2,1)}, bf16[1024,512]{1,0:T(8,128)(2,1)}, f32[16,512]{1,0:T(8,128)}) custom-call(s32[1]{0:T(128)} %bitcast.1.side_ref, s32[2,16]{1,0:T(2,128)} %bitcast.183, s32[1,1024]{1,0:T(1,128)} %bitcast.180, f32[1024,512]{1,0:T(8,128)} %bitcast.169, f32[1024,512]{1,0:T(8,128)} %get-tuple-element.65.first_sum, ...), custom_call_target="tpu_custom_call" | custom-call | flops 16000000000 | bytes 30000000 | tf_op jit(solution)/shard_map/self_back/pallas_call | solution.py:770
  240.7 2.1 convolution_convert_fusion.7
  245.0 4.3 maximum_maximum_fusion
  251.1 2.4 convolution_convert_fusion.5
  253.6 2.4 convolution_convert_fusion.4
  260.1 8.6 %collective-permute-done.13 = bf16[256,512]{1,0:T(8,128)(2,1)} collective-permute-done((bf16[256,512]{1,0:T(8,128)(2,1)S(1)}, bf16[256,512]{1,0:T(8,128)(2,1)}, u32[]{:S(2)}, u32[]{:S(2)}) %collective-permute-start.13) | collective-permute-done | bytes 262176 | tf_op jit(solution)/shard_map/ppermute | solution.py:790
  270.0 8.6 %collective-permute-done.14 = bf16[128,512]{1,0:T(8,128)(2,1)} collective-permute-done((bf16[128,512]{1,0:T(8,128)(2,1)S(1)}, bf16[128,512]{1,0:T(8,128)(2,1)}, u32[]{:S(2)}, u32[]{:S(2)}) %collective-permute-start.14) | collective-permute-done | bytes 131104 | tf_op jit(solution)/shard_map/ppermute | solution.py:790
  279.7 7.9 %collective-permute-done.15 = bf16[128,512]{1,0:T(8,128)(2,1)} collective-permute-done((bf16[128,512]{1,0:T(8,128)(2,1)S(1)}, bf16[128,512]{1,0:T(8,128)(2,1)}, u32[]{:S(2)}, u32[]{:S(2)}) %collective-permute-start.15) | collective-permute-done | bytes 131104 | tf_op jit(solution)/shard_map/ppermute | solution.py:790
  291.9 2.2 fusion.2
  296.6 8.0 %collective-permute-done.16 = bf16[256,512]{1,0:T(8,128)(2,1)} collective-permute-done((bf16[256,512]{1,0:T(8,128)(2,1)}, bf16[256,512]{1,0:T(8,128)(2,1)}, u32[]{:S(2)}, u32[]{:S(2)}) %collective-permute-start.16) | collective-permute-done | bytes 262176 | tf_op jit(solution)/shard_map/ppermute | solution.py:790
  306.4 5.8 %collective-permute-done.4 = bf16[768,512]{1,0:T(8,128)(2,1)} collective-permute-done((bf16[768,512]{1,0:T(8,128)(2,1)}, bf16[768,512]{1,0:T(8,128)(2,1)}, u32[]{:S(2)}, u32[]{:S(2)}) %collective-permute-start.4) | collective-permute-done | bytes 786464 | tf_op jit(solution)/shard_map/ppermute | solution.py:790
  313.7 21.0 %collective-permute-done.21 = bf16[1024,512]{1,0:T(8,128)(2,1)} collective-permute-done((bf16[1024,512]{1,0:T(8,128)(2,1)S(1)}, bf16[1024,512]{1,0:T(8,128)(2,1)}, u32[]{:S(2)}, u32[]{:S(2)}) %collective-permute-start.21) | collective-permute-done | bytes 1048608 | tf_op jit(solution)/shard_map/ppermute | solution.py:790
  336.4 8.6 %collective-permute-done.17 = bf16[512,512]{1,0:T(8,128)(2,1)S(1)} collective-permute-done((bf16[512,512]{1,0:T(8,128)(2,1)S(1)}, bf16[512,512]{1,0:T(8,128)(2,1)S(1)}, u32[]{:S(2)}, u32[]{:S(2)}) %collective-permute-start.17) | collective-permute-done | bytes 524320 | tf_op jit(solution)/shard_map/ppermute | solution.py:790
  345.4 3.4 collective-permute-done.22
  349.0 2.3 collective-permute-start.23
  352.3 10.7 %collective-permute-done.6 = bf16[192,512]{1,0:T(8,128)(2,1)S(1)} collective-permute-done((bf16[192,512]{1,0:T(8,128)(2,1)S(1)}, bf16[192,512]{1,0:T(8,128)(2,1)S(1)}, u32[]{:S(2)}, u32[]{:S(2)}) %collective-permute-start.6) | collective-permute-done | bytes 196640 | tf_op jit(solution)/shard_map/ppermute | solution.py:790
  363.2 9.7 %collective-permute-done.23 = bf16[256,512]{1,0:T(8,128)(2,1)S(1)} collective-permute-done((bf16[256,512]{1,0:T(8,128)(2,1)S(1)}, bf16[256,512]{1,0:T(8,128)(2,1)S(1)}, u32[]{:S(2)}, u32[]{:S(2)}) %collective-permute-start.23) | collective-permute-done | bytes 262176 | tf_op jit(solution)/shard_map/ppermute | solution.py:790
  373.0 9.7 %collective-permute-done.7 = bf16[192,512]{1,0:T(8,128)(2,1)S(1)} collective-permute-done((bf16[192,512]{1,0:T(8,128)(2,1)S(1)}, bf16[192,512]{1,0:T(8,128)(2,1)S(1)}, u32[]{:S(2)}, u32[]{:S(2)}) %collective-permute-start.7) | collective-permute-done | bytes 196640 | tf_op jit(solution)/shard_map/ppermute | solution.py:790
  382.8 4.6 collective-permute-done.24
  388.3 7.5 %collective-permute-done.8 = bf16[384,512]{1,0:T(8,128)(2,1)S(1)} collective-permute-done((bf16[384,512]{1,0:T(8,128)(2,1)S(1)}, bf16[384,512]{1,0:T(8,128)(2,1)S(1)}, u32[]{:S(2)}, u32[]{:S(2)}) %collective-permute-start.8) | collective-permute-done | bytes 393248 | tf_op jit(solution)/shard_map/ppermute | solution.py:790
  397.5 9.6 %collective-permute-done.25 = bf16[512,512]{1,0:T(8,128)(2,1)} collective-permute-done((bf16[512,512]{1,0:T(8,128)(2,1)}, bf16[512,512]{1,0:T(8,128)(2,1)}, u32[]{:S(2)}, u32[]{:S(2)}) %collective-permute-start.25) | collective-permute-done | bytes 524320 | tf_op jit(solution)/shard_map/ppermute | solution.py:790
  410.9 6.8 %collective-permute-done.9 = bf16[768,512]{1,0:T(8,128)(2,1)} collective-permute-done((bf16[768,512]{1,0:T(8,128)(2,1)}, bf16[768,512]{1,0:T(8,128)(2,1)}, u32[]{:S(2)}, u32[]{:S(2)}) %collective-permute-start.9) | collective-permute-done | bytes 786464 | tf_op jit(solution)/shard_map/ppermute | solution.py:790
  419.3 19.7 %collective-permute-done.26 = bf16[1024,512]{1,0:T(8,128)(2,1)S(1)} collective-permute-done((bf16[1024,512]{1,0:T(8,128)(2,1)S(1)}, bf16[1024,512]{1,0:T(8,128)(2,1)S(1)}, u32[]{:S(2)}, u32[]{:S(2)}) %collective-permute-start.26) | collective-permute-done | bytes 1048608 | tf_op jit(solution)/shard_map/ppermute | solution.py:790
  445.0 2.4 copy.38
  450.6 2.1 fusion.10
  452.8 6.4 %bitcast_convert_fusion = (f32[1,2048,512]{2,1,0:T(8,128)}, f32[512,2048]{0,1:T(8,128)}) fusion(bf16[2048,512]{1,0:T(8,128)(2,1)} %collective-permute-done.27, pred[]{:T(512)S(6)} %eq.61, bf16[1024,512]{1,0:T(8,128)(2,1)} %copy-done.4, bf16[1024,512]{1,0:T(8,128)(2,1)S(1)} %copy-done.3), kind=kLoop, calls=%fused_computation.19 | loop fusion | flops 8388608 | bytes 12582913 | tf_op jit(solution)/shard_map/broadcast_in_dim | solution.py:904
  459.1 5.3 %copy.39 = f32[512,2048]{1,0:T(8,128)} copy(f32[512,2048]{0,1:T(8,128)} %get-tuple-element.121) | data formatting | bytes 8388608 | tf_op jit(solution)/shard_map/broadcast_in_dim | solution.py:902
  (141 shorter events, 53.8 us)
Async XLA Ops:
  0.6 6.2 %copy-start.12 = (f32[1,3,512]{2,0,1:T(1,128)S(1)}, f32[1,3,512]{2,0,1:T(1,128)}, u32[]{:S(2)}) copy-start(f32[1,3,512]{2,0,1:T(1,128)} %param.29) | copy-start | bytes 18436
  0.7 6.2 %copy-start.13 = (f32[1,3,512]{2,0,1:T(1,128)S(1)}, f32[1,3,512]{2,0,1:T(1,128)}, u32[]{:S(2)}) copy-start(f32[1,3,512]{2,0,1:T(1,128)} %param.28) | copy-start | bytes 18436
  2.0 48.0 %collective-permute-start.1 = (bf16[1024,512]{1,0:T(8,128)(2,1)S(1)}, bf16[1024,512]{1,0:T(8,128)(2,1)S(1)}, u32[]{:S(2)}, u32[]{:S(2)}) collective-permute-start(bf16[1024,512]{1,0:T(8,128)(2,1)S(1)} %pad_maximum_fusion.4), channel_id=1, source_target_pairs={{0,16},{1,17},{2,18},{3,19},{4,20},{5,21},{6,22},{7,23},{8,24},{9,... | collective-permute-start | bytes 3145736 | tf_op jit(solution)/shard_map/ppermute | solution.py:844
  48.6 24.0 %collective-permute-start = (bf16[1024,512]{1,0:T(8,128)(2,1)}, bf16[1024,512]{1,0:T(8,128)(2,1)S(1)}, u32[]{:S(2)}, u32[]{:S(2)}) collective-permute-start(bf16[1024,512]{1,0:T(8,128)(2,1)} %get-tuple-element.66), channel_id=1, source_target_pairs={{0,16},{1,17},{2,18},{3,19},{4,20},{5,21},{6,22},{7,23},{8,24},{9,... | collective-permute-start | bytes 3145736 | tf_op jit(solution)/shard_map/ppermute | solution.py:848
  74.7 2.9 collective-permute-start.11
  74.8 103.9 %collective-permute-start.2 = (bf16[1024,512]{1,0:T(8,128)(2,1)}, bf16[1024,512]{1,0:T(8,128)(2,1)}, u32[]{:S(2)}, u32[]{:S(2)}) collective-permute-start(bf16[1024,512]{1,0:T(8,128)(2,1)} %get-tuple-element.69), channel_id=1, source_target_pairs={{16,0},{17,1},{18,2},{19,3},{20,4},{21,5},{22,6},{23,7},{24,8},{25... | collective-permute-start | bytes 3145736 | tf_op jit(solution)/shard_map/ppermute | solution.py:856
  80.9 178.1 %collective-permute-start.12 = (bf16[512,512]{1,0:T(8,128)(2,1)}, bf16[512,512]{1,0:T(8,128)(2,1)S(1)}, u32[]{:S(2)}, u32[]{:S(2)}) collective-permute-start(bf16[512,512]{1,0:T(8,128)(2,1)} %dynamic-slice_bitcast_fusion.6), channel_id=1, source_target_pairs={{0,2},{1,3},{2,0},{3,1},{4,6},{5,7},{6,4},{7,5},{8,10},{9,11},{10,... | collective-permute-start | bytes 1572872 | tf_op jit(solution)/shard_map/ppermute | solution.py:790
  206.1 34.6 %copy-start.15 = (bf16[1024,512]{1,0:T(8,128)(2,1)S(1)}, bf16[1024,512]{1,0:T(8,128)(2,1)}, u32[]{:S(2)}) copy-start(bf16[1024,512]{1,0:T(8,128)(2,1)} %get-tuple-element.79.attended) | copy-start | bytes 3145732
  250.7 37.8 %collective-permute-start.3 = (bf16[1536,512]{1,0:T(8,128)(2,1)}, bf16[1536,512]{1,0:T(8,128)(2,1)}, u32[]{:S(2)}, u32[]{:S(2)}) collective-permute-start(bf16[1536,512]{1,0:T(8,128)(2,1)} %dynamic-slice_bitcast_fusion.1), channel_id=1, source_target_pairs={{0,1},{1,0},{2,3},{3,2},{4,5},{5,4},{6,7},{7,6},{8,9},{9,8},{10,11... | collective-permute-start | bytes 4718600 | tf_op jit(solution)/shard_map/ppermute | solution.py:790
  258.9 33.0 %collective-permute-start.20 = (bf16[2048,512]{1,0:T(8,128)(2,1)}, bf16[2048,512]{1,0:T(8,128)(2,1)}, u32[]{:S(2)}, u32[]{:S(2)}) collective-permute-start(bf16[2048,512]{1,0:T(8,128)(2,1)} %dynamic-slice_bitcast_fusion), channel_id=1, source_target_pairs={{0,1},{1,0},{2,3},{3,2},{4,5},{5,4},{6,7},{7,6},{8,9},{9,8},{10,11... | collective-permute-start | bytes 6291464 | tf_op jit(solution)/shard_map/ppermute | solution.py:790
  260.0 8.8 %collective-permute-start.13 = (bf16[256,512]{1,0:T(8,128)(2,1)S(1)}, bf16[256,512]{1,0:T(8,128)(2,1)}, u32[]{:S(2)}, u32[]{:S(2)}) collective-permute-start(bf16[256,512]{1,0:T(8,128)(2,1)S(1)} %dynamic-slice_bitcast_fusion.9), channel_id=1, source_target_pairs={{0,4},{1,5},{2,6},{3,7},{4,0},{5,1},{6,2},{7,3},{8,12},{9,13},{10,... | collective-permute-start | bytes 786440 | tf_op jit(solution)/shard_map/ppermute | solution.py:790
  269.8 8.8 %collective-permute-start.14 = (bf16[128,512]{1,0:T(8,128)(2,1)S(1)}, bf16[128,512]{1,0:T(8,128)(2,1)}, u32[]{:S(2)}, u32[]{:S(2)}) collective-permute-start(bf16[128,512]{1,0:T(8,128)(2,1)S(1)} %dynamic-slice_bitcast_fusion.11), channel_id=1, source_target_pairs={{0,8},{1,9},{2,10},{3,11},{4,12},{5,13},{6,14},{7,15},{8,0},{9,1},... | collective-permute-start | bytes 393224 | tf_op jit(solution)/shard_map/ppermute | solution.py:790
  279.6 7.9 %collective-permute-start.15 = (bf16[128,512]{1,0:T(8,128)(2,1)S(1)}, bf16[128,512]{1,0:T(8,128)(2,1)}, u32[]{:S(2)}, u32[]{:S(2)}) collective-permute-start(bf16[128,512]{1,0:T(8,128)(2,1)S(1)} %fusion.14), channel_id=1, source_target_pairs={{0,8},{1,9},{2,10},{3,11},{4,12},{5,13},{6,14},{7,15},{8,0},{9,1},... | collective-permute-start | bytes 393224 | tf_op jit(solution)/shard_map/ppermute | solution.py:790
  291.5 20.7 %collective-permute-start.4 = (bf16[768,512]{1,0:T(8,128)(2,1)}, bf16[768,512]{1,0:T(8,128)(2,1)}, u32[]{:S(2)}, u32[]{:S(2)}) collective-permute-start(bf16[768,512]{1,0:T(8,128)(2,1)} %dynamic-slice_bitcast_fusion.4), channel_id=1, source_target_pairs={{0,2},{1,3},{2,0},{3,1},{4,6},{5,7},{6,4},{7,5},{8,10},{9,11},{10,... | collective-permute-start | bytes 2359304 | tf_op jit(solution)/shard_map/ppermute | solution.py:790
  294.2 40.5 %collective-permute-start.21 = (bf16[1024,512]{1,0:T(8,128)(2,1)S(1)}, bf16[1024,512]{1,0:T(8,128)(2,1)}, u32[]{:S(2)}, u32[]{:S(2)}) collective-permute-start(bf16[1024,512]{1,0:T(8,128)(2,1)S(1)} %dynamic-slice_bitcast_fusion.2), channel_id=1, source_target_pairs={{0,2},{1,3},{2,0},{3,1},{4,6},{5,7},{6,4},{7,5},{8,10},{9,11},{10,... | collective-permute-start | bytes 3145736 | tf_op jit(solution)/shard_map/ppermute | solution.py:790
  296.6 8.0 %collective-permute-start.16 = (bf16[256,512]{1,0:T(8,128)(2,1)}, bf16[256,512]{1,0:T(8,128)(2,1)}, u32[]{:S(2)}, u32[]{:S(2)}) collective-permute-start(bf16[256,512]{1,0:T(8,128)(2,1)} %pad_maximum_fusion.11), channel_id=1, source_target_pairs={{0,4},{1,5},{2,6},{3,7},{4,0},{5,1},{6,2},{7,3},{8,12},{9,13},{10,... | collective-permute-start | bytes 786440 | tf_op jit(solution)/shard_map/ppermute | solution.py:790
  296.6 15.6 %copy-start.6 = (bf16[1536,512]{1,0:T(8,128)(2,1)S(1)}, bf16[1536,512]{1,0:T(8,128)(2,1)}, u32[]{:S(2)}) copy-start(bf16[1536,512]{1,0:T(8,128)(2,1)} %copy-done.5) | copy-start | bytes 4718596
  305.7 39.2 %collective-permute-start.17 = (bf16[512,512]{1,0:T(8,128)(2,1)S(1)}, bf16[512,512]{1,0:T(8,128)(2,1)S(1)}, u32[]{:S(2)}, u32[]{:S(2)}) collective-permute-start(bf16[512,512]{1,0:T(8,128)(2,1)S(1)} %pad_maximum_fusion.8), channel_id=1, source_target_pairs={{0,2},{1,3},{2,0},{3,1},{4,6},{5,7},{6,4},{7,5},{8,10},{9,11},{10,... | collective-permute-start | bytes 1572872 | tf_op jit(solution)/shard_map/ppermute | solution.py:790
  313.6 31.5 %collective-permute-start.5 = (bf16[384,512]{1,0:T(8,128)(2,1)S(1)}, bf16[384,512]{1,0:T(8,128)(2,1)S(1)}, u32[]{:S(2)}, u32[]{:S(2)}) collective-permute-start(bf16[384,512]{1,0:T(8,128)(2,1)S(1)} %dynamic-slice_bitcast_fusion.7), channel_id=1, source_target_pairs={{0,4},{1,5},{2,6},{3,7},{4,0},{5,1},{6,2},{7,3},{8,12},{9,13},{10,... | collective-permute-start | bytes 1179656 | tf_op jit(solution)/shard_map/ppermute | solution.py:790
  336.3 12.5 %collective-permute-start.22 = (bf16[512,512]{1,0:T(8,128)(2,1)S(1)}, bf16[512,512]{1,0:T(8,128)(2,1)S(1)}, u32[]{:S(2)}, u32[]{:S(2)}) collective-permute-start(bf16[512,512]{1,0:T(8,128)(2,1)S(1)} %dynamic-slice_bitcast_fusion.5), channel_id=1, source_target_pairs={{0,4},{1,5},{2,6},{3,7},{4,0},{5,1},{6,2},{7,3},{8,12},{9,13},{10,... | collective-permute-start | bytes 1572872 | tf_op jit(solution)/shard_map/ppermute | solution.py:790
  345.3 17.7 %collective-permute-start.6 = (bf16[192,512]{1,0:T(8,128)(2,1)S(1)}, bf16[192,512]{1,0:T(8,128)(2,1)S(1)}, u32[]{:S(2)}, u32[]{:S(2)}) collective-permute-start(bf16[192,512]{1,0:T(8,128)(2,1)S(1)} %dynamic-slice_bitcast_fusion.10), channel_id=1, source_target_pairs={{0,8},{1,9},{2,10},{3,11},{4,12},{5,13},{6,14},{7,15},{8,0},{9,1},... | collective-permute-start | bytes 589832 | tf_op jit(solution)/shard_map/ppermute | solution.py:790
  349.0 23.9 %collective-permute-start.23 = (bf16[256,512]{1,0:T(8,128)(2,1)S(1)}, bf16[256,512]{1,0:T(8,128)(2,1)S(1)}, u32[]{:S(2)}, u32[]{:S(2)}) collective-permute-start(bf16[256,512]{1,0:T(8,128)(2,1)S(1)} %dynamic-slice_bitcast_fusion.8), channel_id=1, source_target_pairs={{0,8},{1,9},{2,10},{3,11},{4,12},{5,13},{6,14},{7,15},{8,0},{9,1},... | collective-permute-start | bytes 786440 | tf_op jit(solution)/shard_map/ppermute | solution.py:790
  352.3 56.8 %collective-permute-start.18 = (bf16[1024,512]{1,0:T(8,128)(2,1)}, bf16[1024,512]{1,0:T(8,128)(2,1)S(1)}, u32[]{:S(2)}, u32[]{:S(2)}) collective-permute-start(bf16[1024,512]{1,0:T(8,128)(2,1)} %pad_maximum_fusion.5), channel_id=1, source_target_pairs={{0,1},{1,0},{2,3},{3,2},{4,5},{5,4},{6,7},{7,6},{8,9},{9,8},{10,11... | collective-permute-start | bytes 3145736 | tf_op jit(solution)/shard_map/ppermute | solution.py:790
  363.1 19.6 %collective-permute-start.7 = (bf16[192,512]{1,0:T(8,128)(2,1)S(1)}, bf16[192,512]{1,0:T(8,128)(2,1)S(1)}, u32[]{:S(2)}, u32[]{:S(2)}) collective-permute-start(bf16[192,512]{1,0:T(8,128)(2,1)S(1)} %fusion.13), channel_id=1, source_target_pairs={{0,8},{1,9},{2,10},{3,11},{4,12},{5,13},{6,14},{7,15},{8,0},{9,1},... | collective-permute-start | bytes 589832 | tf_op jit(solution)/shard_map/ppermute | solution.py:790
  372.9 14.5 %collective-permute-start.24 = (bf16[256,512]{1,0:T(8,128)(2,1)S(1)}, bf16[256,512]{1,0:T(8,128)(2,1)S(1)}, u32[]{:S(2)}, u32[]{:S(2)}) collective-permute-start(bf16[256,512]{1,0:T(8,128)(2,1)S(1)} %fusion.11), channel_id=1, source_target_pairs={{0,8},{1,9},{2,10},{3,11},{4,12},{5,13},{6,14},{7,15},{8,0},{9,1},... | collective-permute-start | bytes 786440 | tf_op jit(solution)/shard_map/ppermute | solution.py:790
  382.8 13.1 %collective-permute-start.8 = (bf16[384,512]{1,0:T(8,128)(2,1)S(1)}, bf16[384,512]{1,0:T(8,128)(2,1)S(1)}, u32[]{:S(2)}, u32[]{:S(2)}) collective-permute-start(bf16[384,512]{1,0:T(8,128)(2,1)S(1)} %pad_maximum_fusion.10), channel_id=1, source_target_pairs={{0,4},{1,5},{2,6},{3,7},{4,0},{5,1},{6,2},{7,3},{8,12},{9,13},{10,... | collective-permute-start | bytes 1179656 | tf_op jit(solution)/shard_map/ppermute | solution.py:790
  388.3 18.8 %collective-permute-start.25 = (bf16[512,512]{1,0:T(8,128)(2,1)}, bf16[512,512]{1,0:T(8,128)(2,1)}, u32[]{:S(2)}, u32[]{:S(2)}) collective-permute-start(bf16[512,512]{1,0:T(8,128)(2,1)} %pad_maximum_fusion.9), channel_id=1, source_target_pairs={{0,4},{1,5},{2,6},{3,7},{4,0},{5,1},{6,2},{7,3},{8,12},{9,13},{10,... | collective-permute-start | bytes 1572872 | tf_op jit(solution)/shard_map/ppermute | solution.py:790
  396.9 20.7 %collective-permute-start.9 = (bf16[768,512]{1,0:T(8,128)(2,1)}, bf16[768,512]{1,0:T(8,128)(2,1)}, u32[]{:S(2)}, u32[]{:S(2)}) collective-permute-start(bf16[768,512]{1,0:T(8,128)(2,1)} %pad_maximum_fusion.7), channel_id=1, source_target_pairs={{0,2},{1,3},{2,0},{3,1},{4,6},{5,7},{6,4},{7,5},{8,10},{9,11},{10,... | collective-permute-start | bytes 2359304 | tf_op jit(solution)/shard_map/ppermute | solution.py:790
  408.4 30.6 %collective-permute-start.26 = (bf16[1024,512]{1,0:T(8,128)(2,1)S(1)}, bf16[1024,512]{1,0:T(8,128)(2,1)S(1)}, u32[]{:S(2)}, u32[]{:S(2)}) collective-permute-start(bf16[1024,512]{1,0:T(8,128)(2,1)S(1)} %pad_maximum_fusion.6), channel_id=1, source_target_pairs={{0,2},{1,3},{2,0},{3,1},{4,6},{5,7},{6,4},{7,5},{8,10},{9,11},{10,... | collective-permute-start | bytes 3145736 | tf_op jit(solution)/shard_map/ppermute | solution.py:790
  409.4 32.0 %collective-permute-start.19 = (bf16[1024,512]{1,0:T(8,128)(2,1)S(1)}, bf16[1024,512]{1,0:T(8,128)(2,1)S(1)}, u32[]{:S(2)}, u32[]{:S(2)}) collective-permute-start(bf16[1024,512]{1,0:T(8,128)(2,1)S(1)} %broadcast_select_fusion.3), channel_id=1, source_target_pairs={{16,0},{17,1},{18,2},{19,3},{20,4},{21,5},{22,6},{23,7},{24,8},{25... | collective-permute-start | bytes 3145736 | tf_op jit(solution)/shard_map/ppermute | solution.py:892
  419.2 24.1 %collective-permute-start.10 = (bf16[1536,512]{1,0:T(8,128)(2,1)S(1)}, bf16[1536,512]{1,0:T(8,128)(2,1)S(1)}, u32[]{:S(2)}, u32[]{:S(2)}) collective-permute-start(bf16[1536,512]{1,0:T(8,128)(2,1)S(1)} %pad_maximum_fusion.3), channel_id=1, source_target_pairs={{0,1},{1,0},{2,3},{3,2},{4,5},{5,4},{6,7},{7,6},{8,9},{9,8},{10,11... | collective-permute-start | bytes 4718600 | tf_op jit(solution)/shard_map/ppermute | solution.py:790
  441.4 11.4 %collective-permute-start.27 = (bf16[2048,512]{1,0:T(8,128)(2,1)}, bf16[2048,512]{1,0:T(8,128)(2,1)}, u32[]{:S(2)}, u32[]{:S(2)}) collective-permute-start(bf16[2048,512]{1,0:T(8,128)(2,1)} %pad_maximum_fusion.2), channel_id=1, source_target_pairs={{0,1},{1,0},{2,3},{3,2},{4,5},{5,4},{6,7},{7,6},{8,9},{9,8},{10,11... | collective-permute-start | bytes 6291464 | tf_op jit(solution)/shard_map/ppermute | solution.py:790
  (17 other events, 42.3 us)
